TPU v7x, 32 devices: a whole 2x2x4 slice. The times are simulated.
32 devices in a mesh: grp: 4 (over y, x), aux: 8 (over z, core).
Axes of the slice: x: 2, y: 2, z: 4, core: 2. Of those that a mesh axis runs over, the one named last changes fastest.
Arguments:
- integrals: float32 [1536, 256, 384], P('aux', 'grp'), may hold values from -0.8 to 0.8
- occ_energy: float32 [256], replicated, may hold values from -2 to -0.3
- vir_energy: float32 [384], replicated, may hold values from 0.2 to 3
- orbital_order: int32 [256], replicated, may hold values from 0 to 255, each once
- owners: int32 [1, 4], replicated, may hold values from 0 to 7, as said below
Outputs:
- density: float32 [1536, 256, 384], P('aux', 'grp')
Inputs may be any that keep to these rules, and one draw needn't show every extreme that they name: `orbital_order`: a permutation of the table's entries. owners[s, g] names one of the 8 blocks of the group before g.
All inputs are finite; a program needn't handle non-finite values.
Results may differ from a plain program's by a relative error of at most 0.00011.
Values sent between devices are 32-bit elements; how exact they have to be, the bound alone decides.
No kernel may reach another device: no remote copies, remote signals or barrier semaphores. Data moves between devices by JAX's collectives and lax.ppermute only.
A program may use at most 320 MiB of HBM per device.

v0:
```python
import jax
import jax.numpy as jnp
from jax import lax
from jax.sharding import PartitionSpec as P

level_shift = 0.5


def from_behind(block, axis, distance):
    devices = range(lax.axis_size(axis))
    route = [((i - distance) % len(devices), i) for i in devices]
    return lax.ppermute(block, axis, route)


def body(integrals, occ_energy, vir_energy, orbital_order, owners):
    highest = lax.Precision.HIGHEST
    n_groups = lax.axis_size("grp")
    grp_index = lax.axis_index("grp")
    aux_index = lax.axis_index("aux")
    group_occ = integrals.shape[1]
    n_vir = integrals.shape[2]
    n_occ = occ_energy.shape[0]
    owned = lax.all_to_all(integrals, "aux", split_axis=1, concat_axis=0, tiled=True)
    n_auxfun = owned.shape[0]
    occ_block = owned.shape[1]
    mine_flat = owned.reshape(n_auxfun, occ_block * n_vir)
    onehot = (orbital_order[:, None] == jnp.arange(n_occ, dtype=jnp.int32)[None, :]).astype(
        jnp.float32
    )
    levels = jnp.dot(onehot, occ_energy, precision=highest, preferred_element_type=jnp.float32)
    mine_start = grp_index * group_occ + aux_index * occ_block
    mine_levels = lax.dynamic_slice_in_dim(levels, mine_start, occ_block, 0)
    source_group = (grp_index + n_groups - 1) % n_groups
    my_owners = lax.dynamic_index_in_dim(owners, grp_index, 1, keepdims=False)
    next_group = (grp_index + 1) % n_groups
    next_owners = lax.dynamic_index_in_dim(owners, next_group, 1, keepdims=False)
    pieces = [lax.dynamic_slice_in_dim(integrals, next_owners[0] * occ_block, occ_block, 1)]
    arrived = from_behind(jnp.stack(pieces, 0), "grp", 1)
    gathered = lax.all_gather(arrived, "aux", axis=1, tiled=True)
    vir_pair = vir_energy[None, :, None, None] + vir_energy[None, None, None, :]
    owner_now = my_owners[0]
    j_block = gathered[0]
    j_flat = j_block.reshape(n_auxfun, occ_block * n_vir)
    j_levels = lax.dynamic_slice_in_dim(
        levels, source_group * group_occ + owner_now * occ_block, occ_block, 0
    )
    pair_flat = lax.dot_general(
        mine_flat,
        j_flat,
        (((0,), (0,)), ((), ())),
        precision=highest,
        preferred_element_type=jnp.float32,
    )
    pair_ints = pair_flat.reshape(occ_block, n_vir, occ_block, n_vir)
    swapped = jnp.transpose(pair_ints, (0, 3, 2, 1))
    gaps = vir_pair - mine_levels[:, None, None, None] - j_levels[None, None, :, None] + level_shift
    amplitude = ((2.0 * pair_ints - swapped) / gaps).reshape(occ_block * n_vir, occ_block * n_vir)
    density = lax.dot_general(
        j_flat,
        amplitude,
        (((1,), (1,)), ((), ())),
        precision=highest,
        preferred_element_type=jnp.float32,
    )
    density = density.reshape(n_auxfun, occ_block, n_vir)
    return lax.all_to_all(density, "aux", split_axis=0, concat_axis=1, tiled=True)


def solution(mesh):
    in_specs = (P("aux", "grp", None), P(), P(), P(), P())
    out_specs = P("aux", "grp", None)
    return jax.shard_map(body, mesh=mesh, in_specs=in_specs, out_specs=out_specs, check_vma=False)
```

profile of v0, /device:TPU:0, one launch (start us, length us, event | category | flops | bytes accessed | tf_op | source)
XLA Modules:
  0.0 1671.7 jit_solution(3938637744841911419)
XLA Ops:
  6.5 0.0 copy-start
  6.5 1.4 constant_dynamic-slice_fusion
  8.6 3.2 dynamic-slice_bitcast_fusion
  11.8 2.9 collective-permute-start
  14.7 17.6 %copy.13 = f32[192,64,384]{2,0,1:T(8,128)} copy(f32[192,64,384]{2,1,0:T(8,128)} %param.5) | data formatting | bytes 37748736 | tf_op args[0]
  32.3 0.0 copy-start.4
  32.3 0.0 copy-start.3
  32.3 6.0 all-to-all-start
  38.4 0.0 all-gather.2.cloned.1.call-start
  38.5 28.7 %collective-permute-done = f32[1,192,8,384]{3,2,0,1:T(8,128)S(1)} collective-permute-done((f32[1,192,8,384]{3,2,0,1:T(8,128)}, f32[1,192,8,384]{3,2,0,1:T(8,128)S(1)}, u32[]{:S(2)}, u32[]{:S(2)}) %collective-permute-start) | collective-permute-done | bytes 2359328 | tf_op jit(solution)/shard_map/ppermute | solution.py:12
  67.1 0.0 copy-start.2
  67.1 1.4 copy-done.2
  68.5 0.0 all-gather.2.cloned.1.call-update
  69.2 0.0 copy-done
  69.2 0.0 copy-done.4
  69.2 0.2 fusion.1
  69.5 0.1 fusion.3
  69.6 0.0 copy-done.3
  69.6 0.1 broadcast_add_fusion
  69.7 2.5 broadcast_subtract_fusion
  72.2 526.4 %all-to-all-done = f32[192,64,384]{2,0,1:T(8,128)} async-done(((f32[192,64,384]{2,0,1:T(8,128)}), f32[192,64,384]{2,0,1:T(8,128)}, u32[]{:S(2)}, u32[]{:S(2)}) %all-to-all-start) | async-done | bytes 18874400 | tf_op jit(solution)/shard_map/all_to_all | solution.py:23
  598.7 17.0 %copy.14 = f32[192,8,8,384]{3,2,0,1:T(8,128)S(1)} copy(f32[192,8,8,384]{3,0,2,1:T(8,128)} %bitcast.2) | data formatting | bytes 37748736 | tf_op jit(solution)/shard_map/all_to_all | solution.py:23
  615.7 7.9 copy.20
  623.6 0.0 all-gather.2.cloned.1.call-done
  623.6 17.8 %copy.19 = f32[192,8,8,384]{3,1,2,0:T(8,128)} copy(f32[192,8,8,384]{3,2,1,0:T(8,128)} %bitcast.45) | data formatting | bytes 37748736
  641.4 187.9 %fusion.4 = f32[3072,3072]{1,0:T(8,128)} fusion(f32[1536,3072]{1,0:T(8,128)} %bitcast.50, f32[1536,3072]{1,0:T(8,128)} %bitcast.49), kind=kOutput, calls=%fused_computation.12 | convolution fusion | flops 173946175488 | bytes 75497472 | tf_op jit(solution)/shard_map/dot_general | solution.py:47
  829.4 32.8 %copy.21 = f32[384,8,8,384]{3,2,1,0:T(8,128)} copy(f32[384,8,8,384]{3,1,2,0:T(8,128)} %bitcast.48) | data formatting | bytes 75497472
  862.2 37.0 %copy.15 = f32[8,384,8,384]{3,0,1,2:T(8,128)} copy(f32[8,384,8,384]{1,0,3,2:T(8,128)} %bitcast.43) | data formatting | bytes 75497472 | tf_op jit(solution)/shard_map/reshape | solution.py:54
  899.2 39.4 %fusion = f32[8,384,8,384]{3,0,1,2:T(8,128)} fusion(f32[8,384,8,384]{1,0,3,2:T(8,128)} %bitcast.44, f32[8,384,8,384]{3,0,1,2:T(8,128)} %copy.15, f32[8]{0:T(128)S(1)} %get-tuple-element.6, f32[8,384,384]{2,0,1:T(8,128)} %broadcast_subtract_fusion), kind=kLoop, calls=%fused_computation.1 | loop fusion | flops 47185920 | bytes 117964832 | tf_op jit(solution)/shard_map/div | solution.py:57
  938.6 35.6 %copy.16 = f32[8,384,8,384]{3,2,1,0:T(8,128)} copy(f32[8,384,8,384]{3,0,1,2:T(8,128)} %fusion) | data formatting | bytes 75497472 | tf_op jit(solution)/shard_map/div | solution.py:57
  974.2 40.3 %dot_general.16 = f32[8,384,3072]{2,1,0:T(8,128)} reshape(f32[8,384,8,384]{3,2,1,0:T(8,128)} %copy.16) | data formatting | bytes 75497472 | tf_op jit(solution)/shard_map/dot_general | solution.py:58
  1014.5 20.4 %reshape.61 = f32[1536,3072,1]{1,0,2:T(8,128)} reshape(f32[1,1536,8,384]{3,2,0,1:T(8,128)} %all-gather.2.cloned.1.call-done) | data formatting | bytes 37748736 | tf_op jit(solution)/shard_map/reshape;squeeze | solution.py:43
  1035.0 186.9 %fusion.5 = f32[1536,8,384]{2,0,1:T(8,128)} fusion(f32[1536,3072,1]{1,0,2:T(8,128)} %reshape.61, f32[8,384,3072]{2,1,0:T(8,128)} %dot_general.16), kind=kOutput, calls=%fused_computation.13 | convolution fusion | flops 173946175488 | bytes 75497472 | tf_op jit(solution)/shard_map/dot_general | solution.py:58
  1221.9 23.1 %copy.17 = f32[1536,8,384]{2,1,0:T(8,128)S(1)} copy(f32[1536,8,384]{2,0,1:T(8,128)} %fusion.5) | data formatting | bytes 37748736 | tf_op jit(solution)/shard_map/dot_general | solution.py:58
  1244.9 412.2 %all_to_all.33 = f32[1536,8,384]{2,1,0:T(8,128)S(1)} all-to-all(f32[1536,8,384]{2,1,0:T(8,128)S(1)} %copy.17), channel_id=1, replica_groups=mesh['grp'=4,'aux'=8] {'aux'}, dimensions={0} | all-to-all | bytes 37748736 | tf_op jit(solution)/shard_map/all_to_all | solution.py:66
  1657.2 0.0 copy-start.1
  1657.2 7.2 copy.23
  1664.4 0.0 copy-done.1
Async XLA Ops:
  6.5 62.6 %copy-start = (f32[256]{0:T(256)S(1)}, f32[256]{0:T(256)}, u32[]{:S(2)}) copy-start(f32[256]{0:T(256)} %param.6) | copy-start | bytes 3076
  11.8 55.3 %collective-permute-start = (f32[1,192,8,384]{3,2,0,1:T(8,128)}, f32[1,192,8,384]{3,2,0,1:T(8,128)S(1)}, u32[]{:S(2)}, u32[]{:S(2)}) collective-permute-start(f32[1,192,8,384]{3,2,0,1:T(8,128)} %dynamic-slice_bitcast_fusion), channel_id=1, source_target_pairs={{24,0},{0,8},{8,16},{16,24},{25,1},{1,9},{9,17},{17,25},{26,2},{2,... | collective-permute-start | bytes 7077896 | tf_op jit(solution)/shard_map/ppermute | solution.py:12
  32.3 36.8 %copy-start.4 = (s32[256]{0:T(256)S(1)}, s32[256]{0:T(256)}, u32[]{:S(2)}) copy-start(s32[256]{0:T(256)} %param.8) | copy-start | bytes 3076
  32.3 37.3 %copy-start.3 = (f32[384]{0:T(512)S(1)}, f32[384]{0:T(512)}, u32[]{:S(2)}) copy-start(f32[384]{0:T(512)} %param.7) | copy-start | bytes 4612
  32.3 566.3 %all-to-all-start = ((f32[192,64,384]{2,0,1:T(8,128)}), f32[192,64,384]{2,0,1:T(8,128)}, u32[]{:S(2)}, u32[]{:S(2)}) async-start(f32[192,64,384]{2,0,1:T(8,128)} %copy.13), calls=%async_computation | async-start | bytes 37748736 | tf_op jit(solution)/shard_map/all_to_all | solution.py:23
  38.4 585.2 %all-gather.2.cloned.1.call-start = ((), (), s32[]{:S(2)}) async-start(), calls=%async_computation.2 | async-start | bytes 21233664 | tf_op jit(solution)/shard_map/all_gather | solution.py:39
  67.1 1.4 copy-start.2
  1657.2 7.2 copy-start.1
Sparse Core Ops, SparseCore 0:
  68.7 326.6 all-gather.1
where the time goes:
time: 1680 us; the launch traced here: 1670 us
  waiting for transfers between devices  555 us (33%)
  blocking collectives  412 us (25%)
  matrix products  375 us (22%)
  local copies, waits for them, and re-layouts  263 us (16%)
  other arithmetic  42 us (2%)
    all_to_all x1, waiting for transfers between devices, body(): lax.all_to_all(integrals, 'aux', split_axis=1, concat_axis=0, tiled=True)  526 us
    all_to_all x1, blocking collectives, body(): lax.all_to_all(density, 'aux', split_axis=0, concat_axis=1, tiled=True)  412 us
    dot_general x1, matrix products, body(): lax.dot_general(mine_flat, j_flat, (((0,), (0,)), ((), ())), precision=hi...  188 us
    dot_general x1, matrix products, body(): lax.dot_general(j_flat, amplitude, (((1,), (1,)), ((), ())), precision=hi...  187 us
    unnamed x14, local copies, waits for them, and re-layouts  77.6 us
    dot_general x2, local copies, waits for them, and re-layouts, body(): lax.dot_general(j_flat, amplitude, (((1,), (1,)), ((), ())), precision=hi...  63.4 us
    div x1, other arithmetic, body(): (2.0 * pair_ints - swapped) / gaps  39.4 us
    reshape x1, local copies, waits for them, and re-layouts, body(): pair_ints = pair_flat.reshape(occ_block, n_vir, occ_block, n_vir)  37 us
  transfers between devices with their start and end apart: 3, of which 2 were waited for; matrix products, arithmetic and copies ran while one was open for 3% of the time, Pallas kernels for 0%

commit v1 on v0

v1 whole, which is shorter than its diff:
```python
import jax
import jax.numpy as jnp
from jax import lax
from jax.experimental import pallas as pl
from jax.experimental.pallas import tpu as pltpu
from jax.sharding import PartitionSpec as P

level_shift = 0.5
vmem_bytes = 56 * 1024 * 1024


def from_behind(block, axis, distance):
    devices = range(lax.axis_size(axis))
    route = [((i - distance) % len(devices), i) for i in devices]
    return lax.ppermute(block, axis, route)


def split_bf16(x):
    high = x.astype(jnp.bfloat16)
    low = (x - high.astype(jnp.float32)).astype(jnp.bfloat16)
    return high, low


def dot3(a_high, a_low, b_high, b_low):
    def dot(a, b):
        return jnp.dot(a, b, preferred_element_type=jnp.float32)

    return dot(a_high, b_high) + (dot(a_high, b_low) + dot(a_low, b_high))


def split_j_kernel(j_ref, high_ref, low_ref):
    shards, pair, rows, n_vir = j_ref.shape
    for s in range(shards):
        for q in range(pair):
            high, low = split_bf16(j_ref[s, q])
            at = (0, pl.ds(s * rows, rows), pl.ds(q * n_vir, n_vir))
            high_ref[at] = high
            low_ref[at] = low


def split_j(gathered, pair):
    shards, n_j, rows, n_vir = gathered.shape
    shape = (n_j // pair, shards * rows, pair * n_vir)
    block = pl.BlockSpec((1,) + shape[1:], lambda k: (k, 0, 0))
    return pl.pallas_call(
        split_j_kernel,
        grid=(n_j // pair,),
        in_specs=[pl.BlockSpec((shards, pair, rows, n_vir), lambda k: (0, k, 0, 0))],
        out_specs=[block, block],
        out_shape=[jax.ShapeDtypeStruct(shape, jnp.bfloat16)] * 2,
        compiler_params=pltpu.CompilerParams(vmem_limit_bytes=vmem_bytes),
        name="split_j",
    )(gathered)


def density_kernel(i_levels, j_levels, vir_ref, high_ref, low_ref, b_ref, out_ref,
                   at_high, at_low, amp_high, amp_low):
    shards, n_i, rows, n_vir = b_ref.shape
    n_aux = shards * rows
    pair = high_ref.shape[2] // n_vir
    step = pl.program_id(0)
    merge = 1
    while (merge * rows) % 128 and merge < shards:
        merge *= 2

    @pl.when(step == 0)
    def _():
        for i in range(n_i):
            for s in range(0, shards, merge):
                part = jnp.concatenate([b_ref[s + m, i] for m in range(merge)], 0)
                high, low = split_bf16(part.T)
                at = (pl.ds(i * n_vir, n_vir), pl.ds(s * rows, merge * rows))
                at_high[at] = high
                at_low[at] = low
        out_ref[...] = jnp.zeros_like(out_ref)

    for i in range(n_i):
        mine = pl.ds(i * n_vir, n_vir)
        ints = dot3(at_high[mine, :], at_low[mine, :], high_ref[0], low_ref[0])
        for q in range(pair):
            block = ints[:, q * n_vir:(q + 1) * n_vir]
            gaps = vir_ref[...] - (i_levels[i] + j_levels[step * pair + q])
            high, low = split_bf16((2.0 * block.T - block) / gaps)
            at = (pl.ds(q * n_vir, n_vir), mine)
            amp_high[at] = high
            amp_low[at] = low

    @pl.loop(0, shards // merge)
    def _(s):
        at = pl.ds(pl.multiple_of(s * (merge * rows), merge * rows), merge * rows)
        part = dot3(high_ref[0, at, :], low_ref[0, at, :], amp_high[...], amp_low[...])
        for m in range(merge):
            for i in range(n_i):
                out_ref[s * merge + m, i] += part[m * rows:(m + 1) * rows, i * n_vir:(i + 1) * n_vir]


def block_density(i_levels, j_levels, vir_pair, j_high, j_low, b_block):
    shards, n_i, rows, n_vir = b_block.shape
    steps, n_aux, width = j_high.shape
    whole = lambda shape: pl.BlockSpec(shape, lambda k: (0,) * len(shape))
    smem = pl.BlockSpec(memory_space=pltpu.SMEM)
    j_spec = pl.BlockSpec((1, n_aux, width), lambda k: (k, 0, 0))
    flops = 2 * 2 * 3 * n_aux * n_i * n_vir * steps * width
    return pl.pallas_call(
        density_kernel,
        grid=(steps,),
        in_specs=[smem, smem, whole(vir_pair.shape), j_spec, j_spec, whole(b_block.shape)],
        out_specs=whole(b_block.shape),
        out_shape=jax.ShapeDtypeStruct(b_block.shape, jnp.float32),
        scratch_shapes=[
            pltpu.VMEM((n_i * n_vir, n_aux), jnp.bfloat16),
            pltpu.VMEM((n_i * n_vir, n_aux), jnp.bfloat16),
            pltpu.VMEM((width, n_i * n_vir), jnp.bfloat16),
            pltpu.VMEM((width, n_i * n_vir), jnp.bfloat16),
        ],
        compiler_params=pltpu.CompilerParams(vmem_limit_bytes=vmem_bytes),
        cost_estimate=pl.CostEstimate(
            flops=flops, bytes_accessed=4 * steps * n_aux * width + 8 * b_block.size,
            transcendentals=0),
        name="block_density",
    )(i_levels, j_levels, vir_pair, j_high, j_low, b_block)


def place_kernel(part_ref, *refs):
    out_ref = refs[-1]
    for i in range(part_ref.shape[0]):
        out_ref[:, i, :] = part_ref[i]


def place(part, out, shape, start):
    n_i, rows, n_vir = part.shape
    step = 8 if n_i % 8 == 0 else n_i
    out_block = pl.BlockSpec((rows, step, n_vir), lambda k: (0, start // step + k, 0))
    operands = [part]
    in_specs = [pl.BlockSpec((step, rows, n_vir), lambda k: (k, 0, 0))]
    aliases = {}
    if out is not None:
        operands.append(out)
        in_specs.append(pl.BlockSpec(memory_space=pl.ANY))
        aliases = {1: 0}
    return pl.pallas_call(
        place_kernel,
        grid=(n_i // step,),
        in_specs=in_specs,
        out_specs=out_block,
        out_shape=jax.ShapeDtypeStruct(shape, jnp.float32),
        input_output_aliases=aliases,
        compiler_params=pltpu.CompilerParams(vmem_limit_bytes=vmem_bytes),
        name="place",
    )(*operands)


def body(integrals, occ_energy, vir_energy, orbital_order, owners):
    n_groups = lax.axis_size("grp")
    n_shards = lax.axis_size("aux")
    grp_index = lax.axis_index("grp")
    aux_index = lax.axis_index("aux")
    rows, group_occ, n_vir = integrals.shape
    n_occ = occ_energy.shape[0]
    occ_block = group_occ // n_shards
    n_i = 2 if occ_block % 2 == 0 else 1
    chunk = n_shards * n_i

    onehot = orbital_order[:, None] == jnp.arange(n_occ, dtype=jnp.int32)[None, :]
    levels = jnp.sum(jnp.where(onehot, occ_energy[None, :], 0.0), axis=1)
    vir_pair = vir_energy[:, None] + vir_energy[None, :] + level_shift

    source_group = (grp_index + n_groups - 1) % n_groups
    next_group = (grp_index + 1) % n_groups
    my_owner = lax.dynamic_index_in_dim(owners[0], grp_index, 0, keepdims=False)
    next_owner = lax.dynamic_index_in_dim(owners[0], next_group, 0, keepdims=False)
    sent = lax.dynamic_slice_in_dim(integrals, next_owner * occ_block, occ_block, 1)
    arrived = from_behind(jnp.transpose(sent, (1, 0, 2)), "grp", 1)
    gathered = lax.all_gather(arrived, "aux", axis=0, tiled=False)
    j_levels = lax.dynamic_slice_in_dim(
        levels, source_group * group_occ + my_owner * occ_block, occ_block, 0)
    pair = 2 if occ_block % 2 == 0 else 1

    starts = range(0, group_occ, chunk)
    blocks = []
    for start in starts:
        part = jnp.transpose(integrals[:, start:start + chunk, :], (1, 0, 2))
        part = part.reshape(n_shards, n_i, rows, n_vir)
        blocks.append(lax.all_to_all(part, "aux", split_axis=0, concat_axis=0, tiled=True))
    j_high, j_low = split_j(gathered, pair)
    out = None
    for start, block in zip(starts, blocks):
        i_levels = lax.dynamic_slice_in_dim(
            levels, grp_index * group_occ + start + aux_index * n_i, n_i, 0)
        density = block_density(i_levels, j_levels, vir_pair, j_high, j_low, block)
        back = lax.all_to_all(density, "aux", split_axis=0, concat_axis=0, tiled=True)
        out = place(back.reshape(chunk, rows, n_vir), out, integrals.shape, start)
    return out


def solution(mesh):
    in_specs = (P("aux", "grp", None), P(), P(), P(), P())
    out_specs = P("aux", "grp", None)
    return jax.shard_map(body, mesh=mesh, in_specs=in_specs, out_specs=out_specs, check_vma=False)
```

time: 1680 us -> 1120 us (0.67)
  blocking collectives: 412 us -> 0 us
  matrix products: 375 us -> 0 us
  Pallas kernels: 0 us -> 257 us
  local copies, waits for them, and re-layouts: 263 us -> 58.4 us
  waiting for transfers between devices: 555 us -> 735 us
  other arithmetic: 42 us -> 1.13 us
  starting transfers between devices: 9.03 us -> 41.7 us
    all_to_all x1 -> x0, blocking collectives: 412 us -> none  [body(): lax.all_to_all(density, 'aux', split_axis=0, concat_axis=1, tiled=True)]
    dot_general x3 -> x0, matrix products: 375 us -> none  [the longest x1 188 us: body(): lax.dot_general(mine_flat, j_flat, (((0,), (0,)), ((), ())), precision=hi...]
    pallas_call x0 -> x9, Pallas kernels: none -> 257 us  [the longest x4 225 us: block_density(): pl.pallas_call(density_kernel, grid=(steps,), in_specs=[smem, smem, whole...]
    all_to_all x1 -> x8, waiting for transfers between devices: 526 us -> 683 us  [the longest x4 445 us: body(): lax.all_to_all(part, 'aux', split_axis=0, concat_axis=0, tiled=True)]
    unnamed x14 -> x8, local copies, waits for them, and re-layouts: 77.6 us -> 1.42 us
    dot_general x2 -> x0, local copies, waits for them, and re-layouts: 63.4 us -> none  [body(): lax.dot_general(j_flat, amplitude, (((1,), (1,)), ((), ())), precision=hi...]
    div x1 -> x0, other arithmetic: 39.4 us -> none  [body(): (2.0 * pair_ints - swapped) / gaps]
    reshape x1 -> x0, local copies, waits for them, and re-layouts: 37 us -> none  [body(): pair_ints = pair_flat.reshape(occ_block, n_vir, occ_block, n_vir)]
  transfers between devices with their start and end apart: 3 -> 10, of which waited for: 2 -> 9; matrix products, arithmetic and copies ran while one was open for 3% -> 5% of each run, Pallas kernels for 0% -> 23%
where the time goes in v1:
time: 1120 us; the launch traced here: 1110 us
  waiting for transfers between devices  735 us (66%)
  Pallas kernels  257 us (23%)
  local copies, waits for them, and re-layouts  58.4 us (5%)
  starting transfers between devices  41.7 us (4%)
  between operations  15.1 us (1%)
    all_to_all x4, waiting for transfers between devices, body(): lax.all_to_all(part, 'aux', split_axis=0, concat_axis=0, tiled=True)  445 us
    all_to_all x4, waiting for transfers between devices, body(): lax.all_to_all(density, 'aux', split_axis=0, concat_axis=0, tiled=True)  238 us
    pallas_call x4, Pallas kernels, block_density(): pl.pallas_call(density_kernel, grid=(steps,), in_specs=[smem, smem, whole...  225 us
    ppermute x1, waiting for transfers between devices, from_behind(): return lax.ppermute(block, axis, route)  52.2 us
    transpose x5, local copies, waits for them, and re-layouts, body(): part = jnp.transpose(integrals[:, start:start + chunk, :], (1, 0, 2))  34.9 us
  transfers between devices with their start and end apart: 10, of which 9 were waited for; matrix products, arithmetic and copies ran while one was open for 5% of the time, Pallas kernels for 23%

profile of v1, /device:TPU:0, one launch (start us, length us, event | category | flops | bytes accessed | tf_op | source)
XLA Modules:
  0.0 1108.2 jit_solution(2653131323936864159)
XLA Ops:
  6.5 0.0 all-gather.3.cloned.1.call-start
  6.5 1.3 constant_dynamic-slice_fusion
  8.5 1.8 dynamic-slice_bitcast_fusion
  10.4 3.0 collective-permute-start
  13.3 52.2 %collective-permute-done = f32[8,192,384]{2,0,1:T(8,128)S(1)} collective-permute-done((f32[8,192,384]{2,0,1:T(8,128)S(1)}, f32[8,192,384]{2,0,1:T(8,128)S(1)}, u32[]{:S(2)}, u32[]{:S(2)}) %collective-permute-start) | collective-permute-done | bytes 2359328 | tf_op jit(solution)/shard_map/ppermute | solution.py:15
  65.6 0.0 copy-start
  65.6 1.4 copy-done
  67.0 0.0 all-gather.3.cloned.1.call-update
  67.0 13.2 %slice_bitcast_fusion = (f32[16,192,384]{2,0,1:T(8,128)S(1)}, f32[16,192,384]{2,0,1:T(8,128)}, f32[16,192,384]{2,0,1:T(8,128)}, f32[16,192,384]{2,0,1:T(8,128)}) fusion(f32[192,64,384]{2,1,0:T(8,128)} %param.5), kind=kLoop, calls=%fused_computation | loop fusion | bytes 37748736 | tf_op jit(solution)/shard_map/transpose | solution.py:182
  80.2 3.6 copy.18
  83.8 5.1 all-to-all-start.6
  88.9 6.0 copy.16
  95.0 219.7 %all-to-all-done.6.b_ref = f32[8,2,192,384]{3,2,1,0:T(8,128)} async-done(((f32[8,2,192,384]{3,2,1,0:T(8,128)}), f32[8,2,192,384]{3,2,1,0:T(8,128)}, u32[]{:S(2)}, u32[]{:S(2)}) %all-to-all-start.6) | async-done | bytes 4718624 | tf_op jit(solution)/shard_map/all_to_all | solution.py:184
  314.7 4.7 all-to-all-start.2
  319.3 6.0 copy.15
  325.4 110.7 %all-to-all-done.2.b_ref = f32[8,2,192,384]{3,2,1,0:T(8,128)} async-done(((f32[8,2,192,384]{3,2,1,0:T(8,128)}), f32[8,2,192,384]{3,2,1,0:T(8,128)}, u32[]{:S(2)}, u32[]{:S(2)}) %all-to-all-start.2) | async-done | bytes 4718624 | tf_op jit(solution)/shard_map/all_to_all | solution.py:184
  436.0 4.6 all-to-all-start
  440.7 6.0 copy.17
  446.7 99.2 %all-to-all-done.b_ref = f32[8,2,192,384]{3,2,1,0:T(8,128)} async-done(((f32[8,2,192,384]{3,2,1,0:T(8,128)}), f32[8,2,192,384]{3,2,1,0:T(8,128)}, u32[]{:S(2)}, u32[]{:S(2)}) %all-to-all-start) | async-done | bytes 4718624 | tf_op jit(solution)/shard_map/all_to_all | solution.py:184
  545.9 0.0 copy-start.2
  545.9 0.0 copy-start.3
  545.9 5.3 all-to-all-start.4
  551.8 0.0 copy-done.2
  551.9 0.0 copy-done.3
  551.9 0.2 select_reduce_fusion
  552.0 0.6 dynamic_slice.27.j_levels
  552.7 0.7 fusion
  553.3 0.0 copy-done.1
  553.3 1.0 add_add_fusion.vir_ref
  554.3 17.6 %copy.14 = f32[64,192,384]{2,1,0:T(8,128)} copy(f32[64,192,384]{2,0,1:T(8,128)} %all-gather.3.cloned.1.call-done) | data formatting | bytes 37748736 | tf_op jit(solution)/shard_map/all_gather | solution.py:174
  571.9 13.3 %split_j.1 = (bf16[4,1536,768]{2,1,0:T(8,128)(2,1)}, bf16[4,1536,768]{2,1,0:T(8,128)(2,1)}) custom-call(f32[8,8,192,384]{3,2,1,0:T(8,128)} %bitcast.21), custom_call_target="tpu_custom_call" | custom-call | tf_op jit(solution)/shard_map/split_j/pallas_call | solution.py:45
  585.2 56.3 %block_density.7 = f32[8,2,192,384]{3,2,1,0:T(8,128)} custom-call(f32[2]{0:T(128)} %get-tuple-element.13.i_levels, f32[8]{0:T(128)} %dynamic_slice.27.j_levels, f32[384,384]{1,0:T(8,128)} %add_add_fusion.vir_ref, bf16[4,1536,768]{2,1,0:T(8,128)(2,1)} %get-tuple-element.7.high_ref, bf16[4,1536,768]{2,1,0:T(8,128)(2,1)} %get-tuple-element.8.low_ref, ...), custom_call_target="tpu_custom_call" | custom-call | flops 43486543872 | bytes 28311552 | tf_op jit(solution)/shard_map/block_density/pallas_call | solution.py:104
  641.5 14.9 %all-to-all-done.4.b_ref = f32[8,2,192,384]{3,2,1,0:T(8,128)} async-done(((f32[8,2,192,384]{3,2,1,0:T(8,128)}), f32[8,2,192,384]{3,2,1,0:T(8,128)}, u32[]{:S(2)}, u32[]{:S(2)}) %all-to-all-start.4) | async-done | bytes 4718624 | tf_op jit(solution)/shard_map/all_to_all | solution.py:184
  656.4 4.8 all-to-all-start.7
  661.2 56.3 %block_density.5 = f32[8,2,192,384]{3,2,1,0:T(8,128)} custom-call(f32[2]{0:T(128)} %get-tuple-element.15.i_levels, f32[8]{0:T(128)} %dynamic_slice.27.j_levels, f32[384,384]{1,0:T(8,128)} %add_add_fusion.vir_ref, bf16[4,1536,768]{2,1,0:T(8,128)(2,1)} %get-tuple-element.7.high_ref, bf16[4,1536,768]{2,1,0:T(8,128)(2,1)} %get-tuple-element.8.low_ref, ...), custom_call_target="tpu_custom_call" | custom-call | flops 43486543872 | bytes 28311552 | tf_op jit(solution)/shard_map/block_density/pallas_call | solution.py:104
  717.5 48.9 %all-to-all-done.7 = f32[8,2,192,384]{3,2,1,0:T(8,128)} async-done(((f32[8,2,192,384]{3,2,1,0:T(8,128)}), f32[8,2,192,384]{3,2,1,0:T(8,128)}, u32[]{:S(2)}, u32[]{:S(2)}) %all-to-all-start.7) | async-done | bytes 4718624 | tf_op jit(solution)/shard_map/all_to_all | solution.py:191
  766.4 4.8 all-to-all-start.3
  771.3 56.3 %block_density.6 = f32[8,2,192,384]{3,2,1,0:T(8,128)} custom-call(f32[2]{0:T(128)} %get-tuple-element.14.i_levels, f32[8]{0:T(128)} %dynamic_slice.27.j_levels, f32[384,384]{1,0:T(8,128)} %add_add_fusion.vir_ref, bf16[4,1536,768]{2,1,0:T(8,128)(2,1)} %get-tuple-element.7.high_ref, bf16[4,1536,768]{2,1,0:T(8,128)(2,1)} %get-tuple-element.8.low_ref, ...), custom_call_target="tpu_custom_call" | custom-call | flops 43486543872 | bytes 28311552 | tf_op jit(solution)/shard_map/block_density/pallas_call | solution.py:104
  827.6 48.9 %all-to-all-done.3 = f32[8,2,192,384]{3,2,1,0:T(8,128)} async-done(((f32[8,2,192,384]{3,2,1,0:T(8,128)}), f32[8,2,192,384]{3,2,1,0:T(8,128)}, u32[]{:S(2)}, u32[]{:S(2)}) %all-to-all-start.3) | async-done | bytes 4718624 | tf_op jit(solution)/shard_map/all_to_all | solution.py:191
  876.5 4.8 all-to-all-start.5
  881.4 56.2 %block_density.4 = f32[8,2,192,384]{3,2,1,0:T(8,128)} custom-call(f32[2]{0:T(128)} %get-tuple-element.16.i_levels, f32[8]{0:T(128)} %dynamic_slice.27.j_levels, f32[384,384]{1,0:T(8,128)} %add_add_fusion.vir_ref, bf16[4,1536,768]{2,1,0:T(8,128)(2,1)} %get-tuple-element.7.high_ref, bf16[4,1536,768]{2,1,0:T(8,128)(2,1)} %get-tuple-element.8.low_ref, ...), custom_call_target="tpu_custom_call" | custom-call | flops 43486543872 | bytes 28311552 | tf_op jit(solution)/shard_map/block_density/pallas_call | solution.py:104
  937.6 49.0 %all-to-all-done.5 = f32[8,2,192,384]{3,2,1,0:T(8,128)} async-done(((f32[8,2,192,384]{3,2,1,0:T(8,128)}), f32[8,2,192,384]{3,2,1,0:T(8,128)}, u32[]{:S(2)}, u32[]{:S(2)}) %all-to-all-start.5) | async-done | bytes 4718624 | tf_op jit(solution)/shard_map/all_to_all | solution.py:191
  986.6 4.6 all-to-all-start.1
  991.2 4.6 place.4.refs_0_
  995.8 4.6 place.5.refs_0_
  1000.4 4.6 place.6.refs_0_
  1005.0 91.4 %all-to-all-done.1 = f32[8,2,192,384]{3,2,1,0:T(8,128)} async-done(((f32[8,2,192,384]{3,2,1,0:T(8,128)}), f32[8,2,192,384]{3,2,1,0:T(8,128)}, u32[]{:S(2)}, u32[]{:S(2)}) %all-to-all-start.1) | async-done | bytes 4718624 | tf_op jit(solution)/shard_map/all_to_all | solution.py:191
  1096.5 4.6 place.7
  (2 shorter events, 0.0 us)
Async XLA Ops:
  6.5 547.8 %all-gather.3.cloned.1.call-start = ((), (), s32[]{:S(2)}) async-start(), calls=%async_computation.8 | async-start | bytes 21233664 | tf_op jit(solution)/shard_map/all_gather | solution.py:174
  10.4 55.2 %collective-permute-start = (f32[8,192,384]{2,0,1:T(8,128)S(1)}, f32[8,192,384]{2,0,1:T(8,128)S(1)}, u32[]{:S(2)}, u32[]{:S(2)}) collective-permute-start(f32[8,192,384]{2,0,1:T(8,128)S(1)} %dynamic-slice_bitcast_fusion), channel_id=1, source_target_pairs={{24,0},{0,8},{8,16},{16,24},{25,1},{1,9},{9,17},{17,25},{26,2},{2,... | collective-permute-start | bytes 7077896 | tf_op jit(solution)/shard_map/ppermute | solution.py:15
  65.6 1.4 copy-start
  83.8 230.9 %all-to-all-start.6 = ((f32[8,2,192,384]{3,2,1,0:T(8,128)}), f32[8,2,192,384]{3,2,1,0:T(8,128)}, u32[]{:S(2)}, u32[]{:S(2)}) async-start(f32[8,2,192,384]{3,2,1,0:T(8,128)} %bitcast.25), calls=%async_computation.6 | async-start | bytes 9437184 | tf_op jit(solution)/shard_map/all_to_all | solution.py:184
  314.7 121.4 %all-to-all-start.2 = ((f32[8,2,192,384]{3,2,1,0:T(8,128)}), f32[8,2,192,384]{3,2,1,0:T(8,128)}, u32[]{:S(2)}, u32[]{:S(2)}) async-start(f32[8,2,192,384]{3,2,1,0:T(8,128)} %bitcast.24), calls=%async_computation.2 | async-start | bytes 9437184 | tf_op jit(solution)/shard_map/all_to_all | solution.py:184
  436.0 109.9 %all-to-all-start = ((f32[8,2,192,384]{3,2,1,0:T(8,128)}), f32[8,2,192,384]{3,2,1,0:T(8,128)}, u32[]{:S(2)}, u32[]{:S(2)}) async-start(f32[8,2,192,384]{3,2,1,0:T(8,128)} %bitcast.23), calls=%async_computation | async-start | bytes 9437184 | tf_op jit(solution)/shard_map/all_to_all | solution.py:184
  545.9 5.9 copy-start.2
  545.9 6.0 copy-start.3
  545.9 7.4 copy-start.1
  545.9 110.5 %all-to-all-start.4 = ((f32[8,2,192,384]{3,2,1,0:T(8,128)}), f32[8,2,192,384]{3,2,1,0:T(8,128)}, u32[]{:S(2)}, u32[]{:S(2)}) async-start(f32[8,2,192,384]{3,2,1,0:T(8,128)} %bitcast.22), calls=%async_computation.4 | async-start | bytes 9437184 | tf_op jit(solution)/shard_map/all_to_all | solution.py:184
  656.4 110.0 %all-to-all-start.7 = ((f32[8,2,192,384]{3,2,1,0:T(8,128)}), f32[8,2,192,384]{3,2,1,0:T(8,128)}, u32[]{:S(2)}, u32[]{:S(2)}) async-start(f32[8,2,192,384]{3,2,1,0:T(8,128)} %block_density.7), calls=%async_computation.7 | async-start | bytes 9437184 | tf_op jit(solution)/shard_map/all_to_all | solution.py:191
  766.4 110.1 %all-to-all-start.3 = ((f32[8,2,192,384]{3,2,1,0:T(8,128)}), f32[8,2,192,384]{3,2,1,0:T(8,128)}, u32[]{:S(2)}, u32[]{:S(2)}) async-start(f32[8,2,192,384]{3,2,1,0:T(8,128)} %block_density.5), calls=%async_computation.3 | async-start | bytes 9437184 | tf_op jit(solution)/shard_map/all_to_all | solution.py:191
  876.5 110.1 %all-to-all-start.5 = ((f32[8,2,192,384]{3,2,1,0:T(8,128)}), f32[8,2,192,384]{3,2,1,0:T(8,128)}, u32[]{:S(2)}, u32[]{:S(2)}) async-start(f32[8,2,192,384]{3,2,1,0:T(8,128)} %block_density.6), calls=%async_computation.5 | async-start | bytes 9437184 | tf_op jit(solution)/shard_map/all_to_all | solution.py:191
  986.6 109.9 %all-to-all-start.1 = ((f32[8,2,192,384]{3,2,1,0:T(8,128)}), f32[8,2,192,384]{3,2,1,0:T(8,128)}, u32[]{:S(2)}, u32[]{:S(2)}) async-start(f32[8,2,192,384]{3,2,1,0:T(8,128)} %block_density.4), calls=%async_computation.1 | async-start | bytes 9437184 | tf_op jit(solution)/shard_map/all_to_all | solution.py:191
Sparse Core Ops, SparseCore 0:
  67.1 302.2 all-gather.2

commit v2 on v1

--- a/solution.py
+++ b/solution.py
@@ -121,75 +121,213 @@
     )(i_levels, j_levels, vir_pair, j_high, j_low, b_block)
 
 
-def place_kernel(part_ref, *refs):
+def pack_kernel(at_ref, in_ref, out_ref):
+    for t in range(in_ref.shape[1]):
+        out_ref[t, 0] = in_ref[:, t, :]
+
+
+def pack(integrals, places, width):
+    rows, _, n_vir = integrals.shape
+    n_i = places.shape[0]
+    cuts = 2 if rows % 16 == 0 else 1
+    tile = rows // cuts
+    return pl.pallas_call(
+        pack_kernel,
+        grid_spec=pltpu.PrefetchScalarGridSpec(
+            num_scalar_prefetch=1,
+            grid=(n_i, cuts),
+            in_specs=[pl.BlockSpec((tile, width, n_vir), lambda m, r, at: (r, at[m], 0))],
+            out_specs=pl.BlockSpec((width, 1, tile, n_vir), lambda m, r, at: (0, m, r, 0)),
+        ),
+        out_shape=jax.ShapeDtypeStruct((width, n_i, rows, n_vir), jnp.float32),
+        compiler_params=pltpu.CompilerParams(vmem_limit_bytes=vmem_bytes),
+        cost_estimate=pl.CostEstimate(
+            flops=0, bytes_accessed=8 * width * n_i * rows * n_vir, transcendentals=0),
+        name="pack",
+    )(places, integrals)
+
+
+def place_kernel(at_ref, part_ref, *refs):
     out_ref = refs[-1]
-    for i in range(part_ref.shape[0]):
-        out_ref[:, i, :] = part_ref[i]
-
-
-def place(part, out, shape, start):
-    n_i, rows, n_vir = part.shape
-    step = 8 if n_i % 8 == 0 else n_i
-    out_block = pl.BlockSpec((rows, step, n_vir), lambda k: (0, start // step + k, 0))
-    operands = [part]
-    in_specs = [pl.BlockSpec((step, rows, n_vir), lambda k: (k, 0, 0))]
+    for t in range(part_ref.shape[0]):
+        out_ref[:, t, :] = part_ref[t, 0]
+
+
+def place(part, places, out, shape):
+    width, n_i, rows, n_vir = part.shape
+    cuts = 2 if rows % 16 == 0 else 1
+    tile = rows // cuts
+    operands = [places, part]
+    in_specs = [pl.BlockSpec((width, 1, tile, n_vir), lambda m, r, at: (0, m, r, 0))]
     aliases = {}
     if out is not None:
         operands.append(out)
         in_specs.append(pl.BlockSpec(memory_space=pl.ANY))
-        aliases = {1: 0}
+        aliases = {2: 0}
     return pl.pallas_call(
         place_kernel,
-        grid=(n_i // step,),
-        in_specs=in_specs,
-        out_specs=out_block,
+        grid_spec=pltpu.PrefetchScalarGridSpec(
+            num_scalar_prefetch=1,
+            grid=(n_i, cuts),
+            in_specs=in_specs,
+            out_specs=pl.BlockSpec((tile, width, n_vir), lambda m, r, at: (r, at[m], 0)),
+        ),
         out_shape=jax.ShapeDtypeStruct(shape, jnp.float32),
         input_output_aliases=aliases,
         compiler_params=pltpu.CompilerParams(vmem_limit_bytes=vmem_bytes),
+        cost_estimate=pl.CostEstimate(
+            flops=0, bytes_accessed=8 * width * n_i * rows * n_vir, transcendentals=0),
         name="place",
     )(*operands)
+
+
+def join_j_kernel(at_ref, *refs):
+    high_ref, low_ref = refs[-2:]
+    n_half = (len(refs) - 2) // 3
+    near, cross, late = refs[:n_half], refs[n_half:2 * n_half], refs[2 * n_half:3 * n_half]
+    rows, n_vir = near[0].shape[1:]
+    step = pl.program_id(0)
+    me = at_ref[0]
+    far_start = (1 - me // n_half) * n_half
+
+    def put(x, shard, q):
+        high, low = split_bf16(x)
+        at = (0, pl.ds(pl.multiple_of(shard * rows, rows), rows), pl.ds(q * n_vir, n_vir))
+        high_ref[at] = high
+        low_ref[at] = low
+
+    for q in range(2):
+        @pl.when(step % 2 == q)
+        def _(q=q):
+            for d in range(n_half):
+                put(near[d][0], me ^ d, q)
+
+            @pl.when(step < n_half)
+            def _():
+                for d in range(n_half):
+                    put(cross[d][0], me ^ d ^ n_half, q)
+
+            for d in range(n_half):
+                if d % 2 == q:
+                    @pl.when(step == n_half + d)
+                    def _(d=d):
+                        for s in range(n_half):
+                            put(late[d][s], far_start + s, q)
+
+
+def join_j(me, order, near, cross, late):
+    n_half = len(near)
+    n_j, rows, n_vir = near[0].shape
+    shape = (n_j // 2, 2 * n_half * rows, 2 * n_vir)
+    out_block = pl.BlockSpec((1,) + shape[1:], lambda k, at: (k // 2, 0, 0))
+    in_specs = (
+        [pl.BlockSpec((1, rows, n_vir), lambda k, at: (at[1 + k], 0, 0))] * n_half
+        + [pl.BlockSpec((1, rows, n_vir), lambda k, at: (jnp.minimum(k, n_half - 1), 0, 0))] * n_half
+        + [pl.BlockSpec((n_half, rows, n_vir), lambda k, at: (0, 0, 0))] * n_half
+    )
+    return pl.pallas_call(
+        join_j_kernel,
+        grid_spec=pltpu.PrefetchScalarGridSpec(
+            num_scalar_prefetch=1,
+            grid=(n_j,),
+            in_specs=in_specs,
+            out_specs=[out_block, out_block],
+        ),
+        out_shape=[jax.ShapeDtypeStruct(shape, jnp.bfloat16)] * 2,
+        compiler_params=pltpu.CompilerParams(vmem_limit_bytes=vmem_bytes),
+        cost_estimate=pl.CostEstimate(
+            flops=0, bytes_accessed=8 * n_j * 2 * n_half * rows * n_vir, transcendentals=0),
+        name="join_j",
+    )(jnp.concatenate([me[None], order]), *near, *cross, *late)
+
+
+def across(block, distance):
+    route = [(i, i ^ distance) for i in range(lax.axis_size("aux"))]
+    return lax.ppermute(block, "aux", route)
+
+
+def within_half(block, n_half):
+    found = [block]
+    for d in range(1, n_half):
+        low = d & -d
+        found.append(across(found[d ^ low], low))
+    return found
+
+
+def pick(table, index):
+    chosen = index[:, None] == jnp.arange(table.shape[0], dtype=jnp.int32)[None, :]
+    return jnp.sum(jnp.where(chosen, table[None, :], 0.0), axis=1)
 
 
 def body(integrals, occ_energy, vir_energy, orbital_order, owners):
     n_groups = lax.axis_size("grp")
     n_shards = lax.axis_size("aux")
-    grp_index = lax.axis_index("grp")
-    aux_index = lax.axis_index("aux")
+    grp_index = lax.axis_index("grp").astype(jnp.int32)
+    me = lax.axis_index("aux").astype(jnp.int32)
     rows, group_occ, n_vir = integrals.shape
-    n_occ = occ_energy.shape[0]
     occ_block = group_occ // n_shards
-    n_i = 2 if occ_block % 2 == 0 else 1
-    chunk = n_shards * n_i
-
-    onehot = orbital_order[:, None] == jnp.arange(n_occ, dtype=jnp.int32)[None, :]
-    levels = jnp.sum(jnp.where(onehot, occ_energy[None, :], 0.0), axis=1)
-    vir_pair = vir_energy[:, None] + vir_energy[None, :] + level_shift
+    n_half = n_shards // 2
+    shared = occ_block == n_shards and n_half >= 2 and n_shards & (n_shards - 1) == 0
 
     source_group = (grp_index + n_groups - 1) % n_groups
     next_group = (grp_index + 1) % n_groups
     my_owner = lax.dynamic_index_in_dim(owners[0], grp_index, 0, keepdims=False)
     next_owner = lax.dynamic_index_in_dim(owners[0], next_group, 0, keepdims=False)
+
+    n_blocks = group_occ // n_shards
+    first = next_owner if shared else jnp.int32(0)
+    places = (first + jnp.arange(n_blocks, dtype=jnp.int32)) % n_blocks
+    n_i = 2 if n_blocks % 2 == 0 else 1
+    chunks = [places[m:m + n_i] for m in range(0, n_blocks, n_i)]
+
+    def send_in(part):
+        return lax.all_to_all(part, "aux", split_axis=0, concat_axis=0, tiled=True)
+
+    parts = [pack(integrals, chunk, n_shards) for chunk in chunks]
+    blocks = [send_in(parts[0])]
+
+    def send_after(c, *done):
+        if c < len(parts):
+            part = lax.optimization_barrier((parts[c],) + done)[0]
+            blocks.append(send_in(part))
+
     sent = lax.dynamic_slice_in_dim(integrals, next_owner * occ_block, occ_block, 1)
     arrived = from_behind(jnp.transpose(sent, (1, 0, 2)), "grp", 1)
-    gathered = lax.all_gather(arrived, "aux", axis=0, tiled=False)
-    j_levels = lax.dynamic_slice_in_dim(
-        levels, source_group * group_occ + my_owner * occ_block, occ_block, 0)
-    pair = 2 if occ_block % 2 == 0 else 1
-
-    starts = range(0, group_occ, chunk)
-    blocks = []
-    for start in starts:
-        part = jnp.transpose(integrals[:, start:start + chunk, :], (1, 0, 2))
-        part = part.reshape(n_shards, n_i, rows, n_vir)
-        blocks.append(lax.all_to_all(part, "aux", split_axis=0, concat_axis=0, tiled=True))
-    j_high, j_low = split_j(gathered, pair)
+    natural = jnp.arange(occ_block, dtype=jnp.int32)
+    if shared:
+        half = me // n_half
+        far_start = (1 - half) * n_half
+        near = within_half(arrived, n_half)
+        crossing = lax.dynamic_slice_in_dim(arrived, half * n_half, n_half, 0)
+        crossed = across(crossing, n_half)
+        cross = within_half(crossed, n_half)
+        send_after(1, arrived)
+        owned = lax.dynamic_slice(
+            blocks[0], (far_start, 0, 0, 0), (n_half, 1, rows, n_vir)).reshape(n_half, rows, n_vir)
+        late_own = from_behind(owned, "grp", 1)
+        late = within_half(late_own, n_half)
+        send_after(2, near[n_half // 2], crossed, late_own)
+        send_after(3, *near, *cross, *late)
+        order = jnp.where(natural < n_half, far_start + natural, me ^ (natural - n_half))
+        j_high, j_low = join_j(me, order, near, cross, late)
+    else:
+        order = natural
+        gathered = lax.all_gather(arrived, "aux", axis=0, tiled=False)
+        j_high, j_low = split_j(gathered, 2 if occ_block % 2 == 0 else 1)
+    for c in range(len(blocks), len(parts)):
+        send_after(c)
+
+    levels = pick(occ_energy, orbital_order)
+    vir_pair = vir_energy[:, None] + vir_energy[None, :] + level_shift
+    j_levels = pick(levels, source_group * group_occ + my_owner * occ_block + order)
+    i_levels = pick(levels, grp_index * group_occ + places * n_shards + me)
+
     out = None
-    for start, block in zip(starts, blocks):
-        i_levels = lax.dynamic_slice_in_dim(
-            levels, grp_index * group_occ + start + aux_index * n_i, n_i, 0)
-        density = block_density(i_levels, j_levels, vir_pair, j_high, j_low, block)
+    for c, (chunk, block) in enumerate(zip(chunks, blocks)):
+        density = block_density(
+            i_levels[c * n_i:(c + 1) * n_i], j_levels, vir_pair, j_high, j_low, block)
         back = lax.all_to_all(density, "aux", split_axis=0, concat_axis=0, tiled=True)
-        out = place(back.reshape(chunk, rows, n_vir), out, integrals.shape, start)
+        out = place(back, chunk, out, integrals.shape)
     return out
 
 

time: 1120 us -> 981 us (0.88)
  waiting for transfers between devices: 735 us -> 622 us
  local copies, waits for them, and re-layouts: 58.4 us -> 11.3 us
  Pallas kernels: 257 us -> 292 us
  between operations: 15.1 us -> 1.45 us
    all_to_all x4, waiting for transfers between devices: 445 us -> 76.3 us  [send_in(): return lax.all_to_all(part, 'aux', split_axis=0, concat_axis=0, tiled=True)]
    ppermute x0 -> x10, waiting for transfers between devices: none -> 266 us  [across(): return lax.ppermute(block, 'aux', route)]
    transpose x6 -> x0, local copies, waits for them, and re-layouts: 36.7 us -> none  [the longest x5 34.9 us: body(): part = jnp.transpose(integrals[:, start:start + chunk, :], (1, 0, 2))]
    pallas_call x5 -> x9, Pallas kernels: 31.7 us -> 66.5 us  [the longest x4 25 us: place(): pl.pallas_call(place_kernel, grid_spec=pltpu.PrefetchScalarGridSpec(num_s...]
    all_gather x1 -> x0, local copies, waits for them, and re-layouts: 17.6 us -> none  [body(): gathered = lax.all_gather(arrived, 'aux', axis=0, tiled=False)]
    ppermute x1 -> x2, waiting for transfers between devices: 52.2 us -> 46.8 us  [from_behind(): return lax.ppermute(block, axis, route)]
  transfers between devices with their start and end apart: 10 -> 20, of which waited for: 9 -> 11; matrix products, arithmetic and copies ran while one was open for 5% -> 1% of each run, Pallas kernels for 23% -> 28%
where the time goes in v2:
time: 981 us; the launch traced here: 980 us
  waiting for transfers between devices  622 us (63%)
  Pallas kernels  292 us (30%)
  starting transfers between devices  50.5 us (5%)
  local copies, waits for them, and re-layouts  11.3 us (1%)
    ppermute x10, waiting for transfers between devices, across(): return lax.ppermute(block, 'aux', route)  266 us
    all_to_all x4, waiting for transfers between devices, body(): lax.all_to_all(density, 'aux', split_axis=0, concat_axis=0, tiled=True)  233 us
    pallas_call x4, Pallas kernels, block_density(): pl.pallas_call(density_kernel, grid=(steps,), in_specs=[smem, smem, whole...  225 us
    all_to_all x4, waiting for transfers between devices, send_in(): return lax.all_to_all(part, 'aux', split_axis=0, concat_axis=0, tiled=True)  76.3 us
    ppermute x2, waiting for transfers between devices, from_behind(): return lax.ppermute(block, axis, route)  46.8 us
    pallas_call x4, Pallas kernels, place(): pl.pallas_call(place_kernel, grid_spec=pltpu.PrefetchScalarGridSpec(num_s...  25 us
    pallas_call x4, Pallas kernels, pack(): pl.pallas_call(pack_kernel, grid_spec=pltpu.PrefetchScalarGridSpec(num_sc...  24.9 us
    all_to_all x4, starting transfers between devices, send_in(): return lax.all_to_all(part, 'aux', split_axis=0, concat_axis=0, tiled=True)  20.3 us
  transfers between devices with their start and end apart: 20, of which 11 were waited for; matrix products, arithmetic and copies ran while one was open for 1% of the time, Pallas kernels for 28%

profile of v2, /device:TPU:0, one launch (start us, length us, event | category | flops | bytes accessed | tf_op | source)
XLA Modules:
  0.0 979.5 jit_solution(4298363143727546605)
XLA Ops:
  0.0 1.4 constant_dynamic-slice_fusion.2
  1.9 0.7 fusion.2
  2.6 6.2 pack.4
  8.8 6.3 all-to-all-start
  15.7 1.8 constant_dynamic-slice_fusion.1
  18.0 1.5 collective-permute-start
  19.5 6.2 pack.7
  25.8 46.8 %collective-permute-done.refs_0_ = f32[8,192,384]{2,1,0:T(8,128)S(1)} collective-permute-done((f32[8,192,384]{2,1,0:T(8,128)S(1)}, f32[8,192,384]{2,1,0:T(8,128)S(1)}, u32[]{:S(2)}, u32[]{:S(2)}) %collective-permute-start) | collective-permute-done | bytes 2359328 | tf_op jit(solution)/shard_map/ppermute | solution.py:15
  72.6 47.9 %all-to-all-done.b_ref = f32[8,2,192,384]{3,2,1,0:T(8,128)} async-done(((f32[8,2,192,384]{3,2,1,0:T(8,128)}), f32[8,2,192,384]{3,2,1,0:T(8,128)}, u32[]{:S(2)}, u32[]{:S(2)}) %all-to-all-start) | async-done | bytes 4718624 | tf_op jit(solution)/shard_map/all_to_all | solution.py:284
  120.5 4.6 all-to-all-start.5
  125.1 1.9 collective-permute-start.2
  127.1 2.5 collective-permute-start.4
  129.5 1.3 dynamic-slice_bitcast_fusion
  130.9 1.5 collective-permute-start.8
  132.4 6.2 pack.6
  138.6 139.2 %collective-permute-done.4.refs_4_ = f32[4,192,384]{2,1,0:T(8,128)S(1)} collective-permute-done((f32[4,192,384]{2,1,0:T(8,128)S(1)}, f32[4,192,384]{2,1,0:T(8,128)S(1)}, u32[]{:S(2)}, u32[]{:S(2)}) %collective-permute-start.4) | collective-permute-done | bytes 1179680 | tf_op jit(solution)/shard_map/ppermute | solution.py:246
  277.9 2.1 collective-permute-done.2.refs_2_
  280.0 4.6 all-to-all-start.3
  285.0 2.1 collective-permute-start.6
  287.6 99.4 %collective-permute-done.6.refs_6_ = f32[4,192,384]{2,1,0:T(8,128)S(1)} collective-permute-done((f32[4,192,384]{2,1,0:T(8,128)S(1)}, f32[4,192,384]{2,1,0:T(8,128)S(1)}, u32[]{:S(2)}, u32[]{:S(2)}) %collective-permute-start.6) | collective-permute-done | bytes 1179680 | tf_op jit(solution)/shard_map/ppermute | solution.py:246
  387.1 1.4 copy-done.1
  389.0 25.2 %collective-permute-done.10.refs_10_ = f32[4,192,384]{2,1,0:T(8,128)S(1)} collective-permute-done((f32[4,192,384]{2,1,0:T(8,128)}, f32[4,192,384]{2,1,0:T(8,128)S(1)}, u32[]{:S(2)}, u32[]{:S(2)}) %collective-permute-start.10) | collective-permute-done | bytes 1179680 | tf_op jit(solution)/shard_map/ppermute | solution.py:246
  414.1 6.3 pack.5
  420.5 1.0 copy-done.5
  421.5 1.0 copy-done.6
  422.6 1.0 copy-done.7
  423.9 4.8 all-to-all-start.1
  430.2 0.8 select_reduce_fusion.1
  430.9 0.7 fusion.1
  431.6 1.0 add_add_fusion.vir_ref
  432.5 16.6 %join_j.1 = (bf16[4,1536,768]{2,1,0:T(8,128)(2,1)}, bf16[4,1536,768]{2,1,0:T(8,128)(2,1)}) custom-call(s32[9]{0:T(128)} %pad_add_fusion.at_ref, f32[8,192,384]{2,1,0:T(8,128)} %copy-done, f32[8,192,384]{2,1,0:T(8,128)} %copy-done.1, f32[8,192,384]{2,1,0:T(8,128)} %collective-permute-done.2.refs_2_, f32[8,192,384]{2,1,0:T(8,128)} %collective-permute-done.3.refs_3_, ...), custom_call_target="tpu_custom_call" | custom-call | bytes 37748736 | tf_op jit(solution)/shard_map/join_j/pallas_call | solution.py:228
  449.1 56.3 %block_density.6 = f32[8,2,192,384]{3,2,1,0:T(8,128)} custom-call(f32[2]{0:T(128)} %get-tuple-element.20.i_levels, f32[8]{0:T(128)} %get-tuple-element.15.j_levels, f32[384,384]{1,0:T(8,128)} %add_add_fusion.vir_ref, bf16[4,1536,768]{2,1,0:T(8,128)(2,1)} %get-tuple-element.10.high_ref, bf16[4,1536,768]{2,1,0:T(8,128)(2,1)} %get-tuple-element.11.low_ref, ...), custom_call_target="tpu_custom_call" | custom-call | flops 43486543872 | bytes 28311552 | tf_op jit(solution)/shard_map/block_density/pallas_call | solution.py:104
  505.4 28.4 %all-to-all-done.1.b_ref = f32[8,2,192,384]{3,2,1,0:T(8,128)} async-done(((f32[8,2,192,384]{3,2,1,0:T(8,128)}), f32[8,2,192,384]{3,2,1,0:T(8,128)}, u32[]{:S(2)}, u32[]{:S(2)}) %all-to-all-start.1) | async-done | bytes 4718624 | tf_op jit(solution)/shard_map/all_to_all | solution.py:284
  533.9 4.8 all-to-all-start.6
  538.7 56.2 %block_density.7 = f32[8,2,192,384]{3,2,1,0:T(8,128)} custom-call(f32[2]{0:T(128)} %get-tuple-element.19.i_levels, f32[8]{0:T(128)} %get-tuple-element.15.j_levels, f32[384,384]{1,0:T(8,128)} %add_add_fusion.vir_ref, bf16[4,1536,768]{2,1,0:T(8,128)(2,1)} %get-tuple-element.10.high_ref, bf16[4,1536,768]{2,1,0:T(8,128)(2,1)} %get-tuple-element.11.low_ref, ...), custom_call_target="tpu_custom_call" | custom-call | flops 43486543872 | bytes 28311552 | tf_op jit(solution)/shard_map/block_density/pallas_call | solution.py:104
  594.9 48.8 %all-to-all-done.6.part_ref = f32[8,2,192,384]{3,2,1,0:T(8,128)} async-done(((f32[8,2,192,384]{3,2,1,0:T(8,128)}), f32[8,2,192,384]{3,2,1,0:T(8,128)}, u32[]{:S(2)}, u32[]{:S(2)}) %all-to-all-start.6) | async-done | bytes 4718624 | tf_op jit(solution)/shard_map/all_to_all | solution.py:329
  643.7 4.9 all-to-all-start.7
  648.6 56.3 %block_density.5 = f32[8,2,192,384]{3,2,1,0:T(8,128)} custom-call(f32[2]{0:T(128)} %get-tuple-element.21.i_levels, f32[8]{0:T(128)} %get-tuple-element.15.j_levels, f32[384,384]{1,0:T(8,128)} %add_add_fusion.vir_ref, bf16[4,1536,768]{2,1,0:T(8,128)(2,1)} %get-tuple-element.10.high_ref, bf16[4,1536,768]{2,1,0:T(8,128)(2,1)} %get-tuple-element.11.low_ref, ...), custom_call_target="tpu_custom_call" | custom-call | flops 43486543872 | bytes 28311552 | tf_op jit(solution)/shard_map/block_density/pallas_call | solution.py:104
  704.9 48.7 %all-to-all-done.7.part_ref = f32[8,2,192,384]{3,2,1,0:T(8,128)} async-done(((f32[8,2,192,384]{3,2,1,0:T(8,128)}), f32[8,2,192,384]{3,2,1,0:T(8,128)}, u32[]{:S(2)}, u32[]{:S(2)}) %all-to-all-start.7) | async-done | bytes 4718624 | tf_op jit(solution)/shard_map/all_to_all | solution.py:329
  753.6 4.9 all-to-all-start.4
  758.5 56.2 %block_density.4 = f32[8,2,192,384]{3,2,1,0:T(8,128)} custom-call(f32[2]{0:T(128)} %get-tuple-element.22.i_levels, f32[8]{0:T(128)} %get-tuple-element.15.j_levels, f32[384,384]{1,0:T(8,128)} %add_add_fusion.vir_ref, bf16[4,1536,768]{2,1,0:T(8,128)(2,1)} %get-tuple-element.10.high_ref, bf16[4,1536,768]{2,1,0:T(8,128)(2,1)} %get-tuple-element.11.low_ref, ...), custom_call_target="tpu_custom_call" | custom-call | flops 43486543872 | bytes 28311552 | tf_op jit(solution)/shard_map/block_density/pallas_call | solution.py:104
  814.7 48.7 %all-to-all-done.4.part_ref = f32[8,2,192,384]{3,2,1,0:T(8,128)} async-done(((f32[8,2,192,384]{3,2,1,0:T(8,128)}), f32[8,2,192,384]{3,2,1,0:T(8,128)}, u32[]{:S(2)}, u32[]{:S(2)}) %all-to-all-start.4) | async-done | bytes 4718624 | tf_op jit(solution)/shard_map/all_to_all | solution.py:329
  863.4 4.6 all-to-all-start.2
  868.0 6.2 place.4.refs_0_
  874.3 6.2 place.5.refs_0_
  880.5 6.2 place.6.refs_0_
  886.8 86.5 %all-to-all-done.2.part_ref = f32[8,2,192,384]{3,2,1,0:T(8,128)} async-done(((f32[8,2,192,384]{3,2,1,0:T(8,128)}), f32[8,2,192,384]{3,2,1,0:T(8,128)}, u32[]{:S(2)}, u32[]{:S(2)}) %all-to-all-start.2) | async-done | bytes 4718624 | tf_op jit(solution)/shard_map/all_to_all | solution.py:329
  973.3 6.2 place.7
  (42 shorter events, 3.7 us)
Async XLA Ops:
  8.8 111.7 %all-to-all-start = ((f32[8,2,192,384]{3,2,1,0:T(8,128)}), f32[8,2,192,384]{3,2,1,0:T(8,128)}, u32[]{:S(2)}, u32[]{:S(2)}) async-start(f32[8,2,192,384]{3,2,1,0:T(8,128)} %pack.4), calls=%async_computation | async-start | bytes 9437184 | tf_op jit(solution)/shard_map/all_to_all | solution.py:284
  18.0 54.6 %collective-permute-start = (f32[8,192,384]{2,1,0:T(8,128)S(1)}, f32[8,192,384]{2,1,0:T(8,128)S(1)}, u32[]{:S(2)}, u32[]{:S(2)}) collective-permute-start(f32[8,192,384]{2,1,0:T(8,128)S(1)} %bitcast.8), channel_id=1, source_target_pairs={{24,0},{0,8},{8,16},{16,24},{25,1},{1,9},{9,17},{17,25},{26,2},{2,... | collective-permute-start | bytes 7077896 | tf_op jit(solution)/shard_map/ppermute | solution.py:15
  72.6 212.0 %copy-start = (f32[8,192,384]{2,1,0:T(8,128)}, f32[8,192,384]{2,1,0:T(8,128)S(1)}, u32[]{:S(2)}) copy-start(f32[8,192,384]{2,1,0:T(8,128)S(1)} %collective-permute-done.refs_0_) | copy-start | bytes 7077892
  120.5 159.5 %all-to-all-start.5 = ((f32[8,2,192,384]{3,2,1,0:T(8,128)}), f32[8,2,192,384]{3,2,1,0:T(8,128)}, u32[]{:S(2)}, u32[]{:S(2)}) async-start(f32[8,2,192,384]{3,2,1,0:T(8,128)} %pack.7), calls=%async_computation.5 | async-start | bytes 9437184 | tf_op jit(solution)/shard_map/all_to_all | solution.py:284
  125.1 154.9 %collective-permute-start.2 = (f32[8,192,384]{2,1,0:T(8,128)S(1)}, f32[8,192,384]{2,1,0:T(8,128)}, u32[]{:S(2)}, u32[]{:S(2)}) collective-permute-start(f32[8,192,384]{2,1,0:T(8,128)S(1)} %collective-permute-done.refs_0_), channel_id=1, source_target_pairs={{0,2},{1,3},{2,0},{3,1},{4,6},{5,7},{6,4},{7,5},{8,10},{9,11},{10,... | collective-permute-start | bytes 7077896 | tf_op jit(solution)/shard_map/ppermute | solution.py:246
  127.1 150.8 %collective-permute-start.4 = (f32[4,192,384]{2,1,0:T(8,128)S(1)}, f32[4,192,384]{2,1,0:T(8,128)S(1)}, u32[]{:S(2)}, u32[]{:S(2)}) collective-permute-start(f32[4,192,384]{2,1,0:T(8,128)S(1)} %constant_dynamic-slice_fusion), channel_id=1, source_target_pairs={{0,4},{1,5},{2,6},{3,7},{4,0},{5,1},{6,2},{7,3},{8,12},{9,13},{10,... | collective-permute-start | bytes 3538952 | tf_op jit(solution)/shard_map/ppermute | solution.py:246
  130.9 149.1 %collective-permute-start.8 = (f32[4,192,384]{2,1,0:T(8,128)S(1)}, f32[4,192,384]{2,1,0:T(8,128)}, u32[]{:S(2)}, u32[]{:S(2)}) collective-permute-start(f32[4,192,384]{2,1,0:T(8,128)S(1)} %dynamic-slice_bitcast_fusion), channel_id=1, source_target_pairs={{24,0},{0,8},{8,16},{16,24},{25,1},{1,9},{9,17},{17,25},{26,2},{2,... | collective-permute-start | bytes 3538952 | tf_op jit(solution)/shard_map/ppermute | solution.py:15
  277.8 9.7 copy-start.2
  280.0 142.5 %all-to-all-start.3 = ((f32[8,2,192,384]{3,2,1,0:T(8,128)}), f32[8,2,192,384]{3,2,1,0:T(8,128)}, u32[]{:S(2)}, u32[]{:S(2)}) async-start(f32[8,2,192,384]{3,2,1,0:T(8,128)} %pack.6), calls=%async_computation.3 | async-start | bytes 9437184 | tf_op jit(solution)/shard_map/all_to_all | solution.py:284
  284.6 102.4 %collective-permute-start.1 = (f32[8,192,384]{2,1,0:T(8,128)S(1)}, f32[8,192,384]{2,1,0:T(8,128)S(1)}, u32[]{:S(2)}, u32[]{:S(2)}) collective-permute-start(f32[8,192,384]{2,1,0:T(8,128)S(1)} %collective-permute-done.refs_0_), channel_id=1, source_target_pairs={{0,1},{1,0},{2,3},{3,2},{4,5},{5,4},{6,7},{7,6},{8,9},{9,8},{10,11... | collective-permute-start | bytes 7077896 | tf_op jit(solution)/shard_map/ppermute | solution.py:246
  285.0 102.0 %collective-permute-start.6 = (f32[4,192,384]{2,1,0:T(8,128)S(1)}, f32[4,192,384]{2,1,0:T(8,128)S(1)}, u32[]{:S(2)}, u32[]{:S(2)}) collective-permute-start(f32[4,192,384]{2,1,0:T(8,128)S(1)} %collective-permute-done.4.refs_4_), channel_id=1, source_target_pairs={{0,2},{1,3},{2,0},{3,1},{4,6},{5,7},{6,4},{7,5},{8,10},{9,11},{10,... | collective-permute-start | bytes 3538952 | tf_op jit(solution)/shard_map/ppermute | solution.py:246
  287.1 134.4 %collective-permute-start.3 = (f32[8,192,384]{2,1,0:T(8,128)}, f32[8,192,384]{2,1,0:T(8,128)}, u32[]{:S(2)}, u32[]{:S(2)}) collective-permute-start(f32[8,192,384]{2,1,0:T(8,128)} %collective-permute-done.2.refs_2_), channel_id=1, source_target_pairs={{0,1},{1,0},{2,3},{3,2},{4,5},{5,4},{6,7},{7,6},{8,9},{9,8},{10,11... | collective-permute-start | bytes 7077896 | tf_op jit(solution)/shard_map/ppermute | solution.py:246
  287.3 126.8 %collective-permute-start.10 = (f32[4,192,384]{2,1,0:T(8,128)}, f32[4,192,384]{2,1,0:T(8,128)S(1)}, u32[]{:S(2)}, u32[]{:S(2)}) collective-permute-start(f32[4,192,384]{2,1,0:T(8,128)} %collective-permute-done.8.refs_8_), channel_id=1, source_target_pairs={{0,2},{1,3},{2,0},{3,1},{4,6},{5,7},{6,4},{7,5},{8,10},{9,11},{10,... | collective-permute-start | bytes 3538952 | tf_op jit(solution)/shard_map/ppermute | solution.py:246
  287.6 132.9 %collective-permute-start.5 = (f32[4,192,384]{2,1,0:T(8,128)S(1)}, f32[4,192,384]{2,1,0:T(8,128)S(1)}, u32[]{:S(2)}, u32[]{:S(2)}) collective-permute-start(f32[4,192,384]{2,1,0:T(8,128)S(1)} %collective-permute-done.4.refs_4_), channel_id=1, source_target_pairs={{0,1},{1,0},{2,3},{3,2},{4,5},{5,4},{6,7},{7,6},{8,9},{9,8},{10,11... | collective-permute-start | bytes 3538952 | tf_op jit(solution)/shard_map/ppermute | solution.py:246
  387.0 33.4 %copy-start.3 = (f32[4,192,384]{2,1,0:T(8,128)}, f32[4,192,384]{2,1,0:T(8,128)S(1)}, u32[]{:S(2)}) copy-start(f32[4,192,384]{2,1,0:T(8,128)S(1)} %collective-permute-done.6.refs_6_) | copy-start | bytes 3538948
  387.0 33.4 %collective-permute-start.7 = (f32[4,192,384]{2,1,0:T(8,128)S(1)}, f32[4,192,384]{2,1,0:T(8,128)S(1)}, u32[]{:S(2)}, u32[]{:S(2)}) collective-permute-start(f32[4,192,384]{2,1,0:T(8,128)S(1)} %collective-permute-done.6.refs_6_), channel_id=1, source_target_pairs={{0,1},{1,0},{2,3},{3,2},{4,5},{5,4},{6,7},{7,6},{8,9},{9,8},{10,11... | collective-permute-start | bytes 3538952 | tf_op jit(solution)/shard_map/ppermute | solution.py:246
  387.0 1.4 copy-start.1
  388.5 34.1 %collective-permute-start.9 = (f32[4,192,384]{2,1,0:T(8,128)}, f32[4,192,384]{2,1,0:T(8,128)S(1)}, u32[]{:S(2)}, u32[]{:S(2)}) collective-permute-start(f32[4,192,384]{2,1,0:T(8,128)} %collective-permute-done.8.refs_8_), channel_id=1, source_target_pairs={{0,1},{1,0},{2,3},{3,2},{4,5},{5,4},{6,7},{7,6},{8,9},{9,8},{10,11... | collective-permute-start | bytes 3538952 | tf_op jit(solution)/shard_map/ppermute | solution.py:246
  414.1 6.3 copy-start.4
  414.1 8.4 collective-permute-start.11
  420.4 9.6 copy-start.10
  420.4 9.6 copy-start.11
  420.4 11.2 %copy-start.9 = (f32[384]{0:T(512)S(1)}, f32[384]{0:T(512)}, u32[]{:S(2)}) copy-start(f32[384]{0:T(512)} %param.7) | copy-start | bytes 4612
  420.5 1.0 copy-start.5
  421.5 1.0 copy-start.6
  422.5 1.0 copy-start.7
  422.5 1.4 copy-start.8
  423.9 109.9 %all-to-all-start.1 = ((f32[8,2,192,384]{3,2,1,0:T(8,128)}), f32[8,2,192,384]{3,2,1,0:T(8,128)}, u32[]{:S(2)}, u32[]{:S(2)}) async-start(f32[8,2,192,384]{3,2,1,0:T(8,128)} %pack.5), calls=%async_computation.1 | async-start | bytes 9437184 | tf_op jit(solution)/shard_map/all_to_all | solution.py:284
  533.9 109.9 %all-to-all-start.6 = ((f32[8,2,192,384]{3,2,1,0:T(8,128)}), f32[8,2,192,384]{3,2,1,0:T(8,128)}, u32[]{:S(2)}, u32[]{:S(2)}) async-start(f32[8,2,192,384]{3,2,1,0:T(8,128)} %block_density.6), calls=%async_computation.6 | async-start | bytes 9437184 | tf_op jit(solution)/shard_map/all_to_all | solution.py:329
  643.7 109.8 %all-to-all-start.7 = ((f32[8,2,192,384]{3,2,1,0:T(8,128)}), f32[8,2,192,384]{3,2,1,0:T(8,128)}, u32[]{:S(2)}, u32[]{:S(2)}) async-start(f32[8,2,192,384]{3,2,1,0:T(8,128)} %block_density.7), calls=%async_computation.7 | async-start | bytes 9437184 | tf_op jit(solution)/shard_map/all_to_all | solution.py:329
  753.6 109.9 %all-to-all-start.4 = ((f32[8,2,192,384]{3,2,1,0:T(8,128)}), f32[8,2,192,384]{3,2,1,0:T(8,128)}, u32[]{:S(2)}, u32[]{:S(2)}) async-start(f32[8,2,192,384]{3,2,1,0:T(8,128)} %block_density.5), calls=%async_computation.4 | async-start | bytes 9437184 | tf_op jit(solution)/shard_map/all_to_all | solution.py:329
  863.4 109.8 %all-to-all-start.2 = ((f32[8,2,192,384]{3,2,1,0:T(8,128)}), f32[8,2,192,384]{3,2,1,0:T(8,128)}, u32[]{:S(2)}, u32[]{:S(2)}) async-start(f32[8,2,192,384]{3,2,1,0:T(8,128)} %block_density.4), calls=%async_computation.2 | async-start | bytes 9437184 | tf_op jit(solution)/shard_map/all_to_all | solution.py:329

commit v3 on v2

--- a/solution.py
+++ b/solution.py
@@ -58,7 +58,7 @@
     shards, n_i, rows, n_vir = b_ref.shape
     n_aux = shards * rows
     pair = high_ref.shape[2] // n_vir
-    step = pl.program_id(0)
+    step = pl.program_id(1)
     merge = 1
     while (merge * rows) % 128 and merge < shards:
         merge *= 2
@@ -79,7 +79,7 @@
         ints = dot3(at_high[mine, :], at_low[mine, :], high_ref[0], low_ref[0])
         for q in range(pair):
             block = ints[:, q * n_vir:(q + 1) * n_vir]
-            gaps = vir_ref[...] - (i_levels[i] + j_levels[step * pair + q])
+            gaps = vir_ref[...] - (i_levels[pl.program_id(0) * n_i + i] + j_levels[step * pair + q])
             high, low = split_bf16((2.0 * block.T - block) / gaps)
             at = (pl.ds(q * n_vir, n_vir), mine)
             amp_high[at] = high
@@ -97,21 +97,23 @@
 def block_density(i_levels, j_levels, vir_pair, j_high, j_low, b_block):
     shards, n_i, rows, n_vir = b_block.shape
     steps, n_aux, width = j_high.shape
-    whole = lambda shape: pl.BlockSpec(shape, lambda k: (0,) * len(shape))
+    at_once = 2 if n_i % 2 == 0 else 1
     smem = pl.BlockSpec(memory_space=pltpu.SMEM)
-    j_spec = pl.BlockSpec((1, n_aux, width), lambda k: (k, 0, 0))
+    vir_spec = pl.BlockSpec(vir_pair.shape, lambda h, k: (0, 0))
+    j_spec = pl.BlockSpec((1, n_aux, width), lambda h, k: (k, 0, 0))
+    b_spec = pl.BlockSpec((shards, at_once, rows, n_vir), lambda h, k: (0, h, 0, 0))
     flops = 2 * 2 * 3 * n_aux * n_i * n_vir * steps * width
     return pl.pallas_call(
         density_kernel,
-        grid=(steps,),
-        in_specs=[smem, smem, whole(vir_pair.shape), j_spec, j_spec, whole(b_block.shape)],
-        out_specs=whole(b_block.shape),
+        grid=(n_i // at_once, steps),
+        in_specs=[smem, smem, vir_spec, j_spec, j_spec, b_spec],
+        out_specs=b_spec,
         out_shape=jax.ShapeDtypeStruct(b_block.shape, jnp.float32),
         scratch_shapes=[
-            pltpu.VMEM((n_i * n_vir, n_aux), jnp.bfloat16),
-            pltpu.VMEM((n_i * n_vir, n_aux), jnp.bfloat16),
-            pltpu.VMEM((width, n_i * n_vir), jnp.bfloat16),
-            pltpu.VMEM((width, n_i * n_vir), jnp.bfloat16),
+            pltpu.VMEM((at_once * n_vir, n_aux), jnp.bfloat16),
+            pltpu.VMEM((at_once * n_vir, n_aux), jnp.bfloat16),
+            pltpu.VMEM((width, at_once * n_vir), jnp.bfloat16),
+            pltpu.VMEM((width, at_once * n_vir), jnp.bfloat16),
         ],
         compiler_params=pltpu.CompilerParams(vmem_limit_bytes=vmem_bytes),
         cost_estimate=pl.CostEstimate(
@@ -278,21 +280,25 @@
     first = next_owner if shared else jnp.int32(0)
     places = (first + jnp.arange(n_blocks, dtype=jnp.int32)) % n_blocks
     n_i = 2 if n_blocks % 2 == 0 else 1
-    chunks = [places[m:m + n_i] for m in range(0, n_blocks, n_i)]
+    ends = [0, n_i, n_blocks - n_i, n_blocks] if n_blocks >= 3 * n_i else [0, n_blocks]
+    chunks = [places[start:end] for start, end in zip(ends, ends[1:])]
 
     def send_in(part):
         return lax.all_to_all(part, "aux", split_axis=0, concat_axis=0, tiled=True)
 
     parts = [pack(integrals, chunk, n_shards) for chunk in chunks]
     blocks = [send_in(parts[0])]
+    sent = lax.dynamic_slice_in_dim(integrals, next_owner * occ_block, occ_block, 1)
+    arrived = from_behind(jnp.transpose(sent, (1, 0, 2)), "grp", 1)
+    if len(parts) > 1:
+        bound = lax.optimization_barrier((arrived, *parts[1:]))
+        arrived, parts[1:] = bound[0], bound[1:]
 
     def send_after(c, *done):
         if c < len(parts):
-            part = lax.optimization_barrier((parts[c],) + done)[0]
+            part = lax.optimization_barrier((parts[c], blocks[c - 1]) + done)[0]
             blocks.append(send_in(part))
 
-    sent = lax.dynamic_slice_in_dim(integrals, next_owner * occ_block, occ_block, 1)
-    arrived = from_behind(jnp.transpose(sent, (1, 0, 2)), "grp", 1)
     natural = jnp.arange(occ_block, dtype=jnp.int32)
     if shared:
         half = me // n_half
@@ -300,14 +306,14 @@
         near = within_half(arrived, n_half)
         crossing = lax.dynamic_slice_in_dim(arrived, half * n_half, n_half, 0)
         crossed = across(crossing, n_half)
-        cross = within_half(crossed, n_half)
-        send_after(1, arrived)
+        send_after(1, near[n_half // 2], crossed)
         owned = lax.dynamic_slice(
             blocks[0], (far_start, 0, 0, 0), (n_half, 1, rows, n_vir)).reshape(n_half, rows, n_vir)
         late_own = from_behind(owned, "grp", 1)
+        crossed = lax.optimization_barrier((crossed, late_own))[0]
+        cross = within_half(crossed, n_half)
         late = within_half(late_own, n_half)
-        send_after(2, near[n_half // 2], crossed, late_own)
-        send_after(3, *near, *cross, *late)
+        send_after(2, *near, *cross, *late)
         order = jnp.where(natural < n_half, far_start + natural, me ^ (natural - n_half))
         j_high, j_low = join_j(me, order, near, cross, late)
     else:
@@ -325,7 +331,8 @@
     out = None
     for c, (chunk, block) in enumerate(zip(chunks, blocks)):
         density = block_density(
-            i_levels[c * n_i:(c + 1) * n_i], j_levels, vir_pair, j_high, j_low, block)
+            i_levels[ends[c]:ends[c + 1]], j_levels, vir_pair, j_high, j_low, block)
+        density = lax.optimization_barrier((density, blocks[-1]))[0]
         back = lax.all_to_all(density, "aux", split_axis=0, concat_axis=0, tiled=True)
         out = place(back, chunk, out, integrals.shape)
     return out

time: 981 us -> 938 us (0.956)
  waiting for transfers between devices: 622 us -> 597 us
    all_to_all x4 -> x3, waiting for transfers between devices: 76.3 us -> 29.3 us  [send_in(): return lax.all_to_all(part, 'aux', split_axis=0, concat_axis=0, tiled=True)]
    ppermute x2, waiting for transfers between devices: 46.8 us -> 62.6 us  [from_behind(): return lax.ppermute(block, axis, route)]
    pallas_call x4 -> x3, Pallas kernels: 225 us -> 219 us  [block_density(): pl.pallas_call(density_kernel, grid=(n_i // at_once, steps), in_specs=[sm...]
    all_to_all x4 -> x3, waiting for transfers between devices: 233 us -> 238 us  [body(): lax.all_to_all(density, 'aux', split_axis=0, concat_axis=0, tiled=True)]
    all_to_all x4 -> x3, starting transfers between devices: 20.3 us -> 17.1 us  [send_in(): return lax.all_to_all(part, 'aux', split_axis=0, concat_axis=0, tiled=True)]
    pallas_call x4 -> x3, Pallas kernels: 24.9 us -> 23.7 us  [pack(): pl.pallas_call(pack_kernel, grid_spec=pltpu.PrefetchScalarGridSpec(num_sc...]
    pallas_call x4 -> x3, Pallas kernels: 25 us -> 23.8 us  [place(): pl.pallas_call(place_kernel, grid_spec=pltpu.PrefetchScalarGridSpec(num_s...]
  transfers between devices with their start and end apart: 20 -> 18, of which waited for: 11 -> 11; matrix products, arithmetic and copies ran while one was open for 1% -> 1% of each run, Pallas kernels for 28% -> 29%
where the time goes in v3:
time: 938 us; the launch traced here: 936 us
  waiting for transfers between devices  597 us (64%)
  Pallas kernels  283 us (30%)
  starting transfers between devices  41.6 us (4%)
  local copies, waits for them, and re-layouts  10.3 us (1%)
    ppermute x10, waiting for transfers between devices, across(): return lax.ppermute(block, 'aux', route)  267 us
    all_to_all x3, waiting for transfers between devices, body(): lax.all_to_all(density, 'aux', split_axis=0, concat_axis=0, tiled=True)  238 us
    pallas_call x3, Pallas kernels, block_density(): pl.pallas_call(density_kernel, grid=(n_i // at_once, steps), in_specs=[sm...  219 us
    ppermute x2, waiting for transfers between devices, from_behind(): return lax.ppermute(block, axis, route)  62.6 us
    all_to_all x3, waiting for transfers between devices, send_in(): return lax.all_to_all(part, 'aux', split_axis=0, concat_axis=0, tiled=True)  29.3 us
    pallas_call x3, Pallas kernels, place(): pl.pallas_call(place_kernel, grid_spec=pltpu.PrefetchScalarGridSpec(num_s...  23.8 us
    pallas_call x3, Pallas kernels, pack(): pl.pallas_call(pack_kernel, grid_spec=pltpu.PrefetchScalarGridSpec(num_sc...  23.7 us
  transfers between devices with their start and end apart: 18, of which 11 were waited for; matrix products, arithmetic and copies ran while one was open for 1% of the time, Pallas kernels for 29%

profile of v3, /device:TPU:0, one launch (start us, length us, event | category | flops | bytes accessed | tf_op | source)
XLA Modules:
  0.0 936.2 jit_solution(5478016641632215973)
XLA Ops:
  0.0 1.4 constant_dynamic-slice_fusion.2
  1.4 0.7 and_select_fusion
  2.0 0.6 fusion.2
  2.6 6.2 pack.5
  8.9 6.3 all-to-all-start
  15.9 1.8 constant_dynamic-slice_fusion.1
  17.7 0.5 copy.12
  18.1 1.5 collective-permute-start
  19.7 0.6 slice.20.at_ref
  20.3 6.2 pack.4
  26.5 11.2 %pack.3 = f32[8,4,192,384]{3,2,1,0:T(8,128)} custom-call(s32[4]{0:T(128)} %slice.20.at_ref, f32[192,64,384]{2,1,0:T(8,128)} %in_ref.5), custom_call_target="tpu_custom_call" | custom-call | bytes 18874368 | tf_op jit(solution)/shard_map/pack/pallas_call | solution.py:136
  37.7 35.0 %collective-permute-done.refs_0_ = f32[8,192,384]{2,1,0:T(8,128)S(1)} collective-permute-done((f32[8,192,384]{2,1,0:T(8,128)S(1)}, f32[8,192,384]{2,1,0:T(8,128)S(1)}, u32[]{:S(2)}, u32[]{:S(2)}) %collective-permute-start) | collective-permute-done | bytes 2359328 | tf_op jit(solution)/shard_map/ppermute | solution.py:15
  72.8 1.7 collective-permute-start.2
  74.5 2.4 collective-permute-start.4
  76.9 91.1 %collective-permute-done.4.refs_4_ = f32[4,192,384]{2,1,0:T(8,128)S(1)} collective-permute-done((f32[4,192,384]{2,1,0:T(8,128)S(1)}, f32[4,192,384]{2,1,0:T(8,128)S(1)}, u32[]{:S(2)}, u32[]{:S(2)}) %collective-permute-start.4) | collective-permute-done | bytes 1179680 | tf_op jit(solution)/shard_map/ppermute | solution.py:248
  168.0 5.7 collective-permute-done.2.refs_2_
  173.8 5.1 all-to-all-start.1
  178.8 1.4 dynamic-slice_bitcast_fusion
  180.2 1.1 collective-permute-start.5
  181.4 0.4 collective-permute-start.3
  181.9 27.6 %collective-permute-done.5.refs_8_ = f32[4,192,384]{2,1,0:T(8,128)S(1)} collective-permute-done((f32[4,192,384]{2,1,0:T(8,128)S(1)}, f32[4,192,384]{2,1,0:T(8,128)S(1)}, u32[]{:S(2)}, u32[]{:S(2)}) %collective-permute-start.5) | collective-permute-done | bytes 1179680 | tf_op jit(solution)/shard_map/ppermute | solution.py:15
  209.4 1.7 collective-permute-start.10
  211.1 0.4 collective-permute-start.7
  211.5 1.4 copy-done.1
  212.9 0.5 collective-permute-start.9
  213.4 143.7 %collective-permute-done.10.refs_10_ = f32[4,192,384]{2,1,0:T(8,128)S(1)} collective-permute-done((f32[4,192,384]{2,1,0:T(8,128)S(1)}, f32[4,192,384]{2,1,0:T(8,128)S(1)}, u32[]{:S(2)}, u32[]{:S(2)}) %collective-permute-start.10) | collective-permute-done | bytes 1179680 | tf_op jit(solution)/shard_map/ppermute | solution.py:248
  357.1 25.0 %collective-permute-done.7.refs_6_ = f32[4,192,384]{2,1,0:T(8,128)S(1)} collective-permute-done((f32[4,192,384]{2,1,0:T(8,128)S(1)}, f32[4,192,384]{2,1,0:T(8,128)S(1)}, u32[]{:S(2)}, u32[]{:S(2)}) %collective-permute-start.7) | collective-permute-done | bytes 1179680 | tf_op jit(solution)/shard_map/ppermute | solution.py:248
  382.2 1.3 copy-done.5
  383.5 1.6 collective-permute-done.8.refs_7_
  385.2 5.7 all-to-all-start.2
  391.6 0.6 pad_add_fusion.at_ref
  392.4 0.8 select_reduce_fusion.1
  393.2 0.7 fusion.1
  393.8 0.9 add_add_fusion.vir_ref
  394.8 16.6 %join_j.1 = (bf16[4,1536,768]{2,1,0:T(8,128)(2,1)}, bf16[4,1536,768]{2,1,0:T(8,128)(2,1)}) custom-call(s32[9]{0:T(128)} %pad_add_fusion.at_ref, f32[8,192,384]{2,1,0:T(8,128)} %copy-done, f32[8,192,384]{2,1,0:T(8,128)} %copy-done.1, f32[8,192,384]{2,1,0:T(8,128)} %collective-permute-done.2.refs_2_, f32[8,192,384]{2,1,0:T(8,128)} %collective-permute-done.3.refs_3_, ...), custom_call_target="tpu_custom_call" | custom-call | bytes 37748736 | tf_op jit(solution)/shard_map/join_j/pallas_call | solution.py:230
  411.3 56.1 %block_density.5 = f32[8,2,192,384]{3,2,1,0:T(8,128)} custom-call(f32[2]{0:T(128)} %get-tuple-element.31.i_levels, f32[8]{0:T(128)} %get-tuple-element.27.j_levels, f32[384,384]{1,0:T(8,128)} %add_add_fusion.vir_ref, bf16[4,1536,768]{2,1,0:T(8,128)(2,1)} %get-tuple-element.18.high_ref, bf16[4,1536,768]{2,1,0:T(8,128)(2,1)} %get-tuple-element.19.low_ref, ...), custom_call_target="tpu_custom_call" | custom-call | flops 43486543872 | bytes 28311552 | tf_op jit(solution)/shard_map/block_density/pallas_call | solution.py:106
  467.5 29.3 %all-to-all-done.2.b_ref = f32[8,2,192,384]{3,2,1,0:T(8,128)} async-done(((f32[8,2,192,384]{3,2,1,0:T(8,128)}), f32[8,2,192,384]{3,2,1,0:T(8,128)}, u32[]{:S(2)}, u32[]{:S(2)}) %all-to-all-start.2) | async-done | bytes 4718624 | tf_op jit(solution)/shard_map/all_to_all | solution.py:287
  496.7 4.8 all-to-all-start.5
  501.6 0.6 slice.22.i_levels
  502.2 106.5 %block_density.4 = f32[8,4,192,384]{3,2,1,0:T(8,128)} custom-call(f32[4]{0:T(128)} %slice.22.i_levels, f32[8]{0:T(128)} %get-tuple-element.27.j_levels, f32[384,384]{1,0:T(8,128)} %add_add_fusion.vir_ref, bf16[4,1536,768]{2,1,0:T(8,128)(2,1)} %get-tuple-element.18.high_ref, bf16[4,1536,768]{2,1,0:T(8,128)(2,1)} %get-tuple-element.19.low_ref, ...), custom_call_target="tpu_custom_call" | custom-call | flops 86973087744 | bytes 37748736 | tf_op jit(solution)/shard_map/block_density/pallas_call | solution.py:106
  608.7 5.3 all-to-all-start.4
  614.0 56.1 %block_density.3 = f32[8,2,192,384]{3,2,1,0:T(8,128)} custom-call(f32[2]{0:T(128)} %get-tuple-element.32.i_levels, f32[8]{0:T(128)} %get-tuple-element.27.j_levels, f32[384,384]{1,0:T(8,128)} %add_add_fusion.vir_ref, bf16[4,1536,768]{2,1,0:T(8,128)(2,1)} %get-tuple-element.18.high_ref, bf16[4,1536,768]{2,1,0:T(8,128)(2,1)} %get-tuple-element.19.low_ref, ...), custom_call_target="tpu_custom_call" | custom-call | flops 43486543872 | bytes 28311552 | tf_op jit(solution)/shard_map/block_density/pallas_call | solution.py:106
  670.1 150.0 %all-to-all-done.4.part_ref = f32[8,4,192,384]{3,2,1,0:T(8,128)} async-done(((f32[8,4,192,384]{3,2,1,0:T(8,128)}), f32[8,4,192,384]{3,2,1,0:T(8,128)}, u32[]{:S(2)}, u32[]{:S(2)}) %all-to-all-start.4) | async-done | bytes 9437216 | tf_op jit(solution)/shard_map/all_to_all | solution.py:336
  820.1 4.6 all-to-all-start.3
  824.7 6.2 place.3.refs_0_
  830.9 11.3 %place.4.refs_0_ = f32[192,64,384]{2,1,0:T(8,128)} custom-call(s32[4]{0:T(128)} %slice.20.at_ref, f32[8,4,192,384]{3,2,1,0:T(8,128)} %all-to-all-done.4.part_ref, f32[192,64,384]{2,1,0:T(8,128)} %place.3.refs_0_), custom_call_target="tpu_custom_call", output_to_operand_aliasing={{}: (2, {})} | custom-call | bytes 18874368 | tf_op jit(solution)/shard_map/place/pallas_call | solution.py:169
  842.2 87.7 %all-to-all-done.3.part_ref = f32[8,2,192,384]{3,2,1,0:T(8,128)} async-done(((f32[8,2,192,384]{3,2,1,0:T(8,128)}), f32[8,2,192,384]{3,2,1,0:T(8,128)}, u32[]{:S(2)}, u32[]{:S(2)}) %all-to-all-start.3) | async-done | bytes 4718624 | tf_op jit(solution)/shard_map/all_to_all | solution.py:336
  929.9 6.2 place.5
  (37 shorter events, 0.5 us)
Async XLA Ops:
  8.9 164.9 %all-to-all-start = ((f32[8,2,192,384]{3,2,1,0:T(8,128)}), f32[8,2,192,384]{3,2,1,0:T(8,128)}, u32[]{:S(2)}, u32[]{:S(2)}) async-start(f32[8,2,192,384]{3,2,1,0:T(8,128)} %pack.5), calls=%async_computation | async-start | bytes 9437184 | tf_op jit(solution)/shard_map/all_to_all | solution.py:287
  18.1 54.6 %collective-permute-start = (f32[8,192,384]{2,1,0:T(8,128)S(1)}, f32[8,192,384]{2,1,0:T(8,128)S(1)}, u32[]{:S(2)}, u32[]{:S(2)}) collective-permute-start(f32[8,192,384]{2,1,0:T(8,128)S(1)} %bitcast.8), channel_id=1, source_target_pairs={{24,0},{0,8},{8,16},{16,24},{25,1},{1,9},{9,17},{17,25},{26,2},{2,... | collective-permute-start | bytes 7077896 | tf_op jit(solution)/shard_map/ppermute | solution.py:15
  72.8 108.6 %copy-start = (f32[8,192,384]{2,1,0:T(8,128)}, f32[8,192,384]{2,1,0:T(8,128)S(1)}, u32[]{:S(2)}) copy-start(f32[8,192,384]{2,1,0:T(8,128)S(1)} %collective-permute-done.refs_0_) | copy-start | bytes 7077892
  72.8 101.0 %collective-permute-start.2 = (f32[8,192,384]{2,1,0:T(8,128)S(1)}, f32[8,192,384]{2,1,0:T(8,128)}, u32[]{:S(2)}, u32[]{:S(2)}) collective-permute-start(f32[8,192,384]{2,1,0:T(8,128)S(1)} %collective-permute-done.refs_0_), channel_id=1, source_target_pairs={{0,2},{1,3},{2,0},{3,1},{4,6},{5,7},{6,4},{7,5},{8,10},{9,11},{10,... | collective-permute-start | bytes 7077896 | tf_op jit(solution)/shard_map/ppermute | solution.py:248
  74.5 93.5 %collective-permute-start.4 = (f32[4,192,384]{2,1,0:T(8,128)S(1)}, f32[4,192,384]{2,1,0:T(8,128)S(1)}, u32[]{:S(2)}, u32[]{:S(2)}) collective-permute-start(f32[4,192,384]{2,1,0:T(8,128)S(1)} %constant_dynamic-slice_fusion), channel_id=1, source_target_pairs={{0,4},{1,5},{2,6},{3,7},{4,0},{5,1},{6,2},{7,3},{8,12},{9,13},{10,... | collective-permute-start | bytes 3538952 | tf_op jit(solution)/shard_map/ppermute | solution.py:248
  168.0 43.4 %copy-start.2 = (f32[4,192,384]{2,1,0:T(8,128)}, f32[4,192,384]{2,1,0:T(8,128)S(1)}, u32[]{:S(2)}) copy-start(f32[4,192,384]{2,1,0:T(8,128)S(1)} %collective-permute-done.4.refs_4_) | copy-start | bytes 3538948
  173.8 211.4 %all-to-all-start.1 = ((f32[8,4,192,384]{3,2,1,0:T(8,128)}), f32[8,4,192,384]{3,2,1,0:T(8,128)}, u32[]{:S(2)}, u32[]{:S(2)}) async-start(f32[8,4,192,384]{3,2,1,0:T(8,128)} %pack.3), calls=%async_computation.1 | async-start | bytes 18874368 | tf_op jit(solution)/shard_map/all_to_all | solution.py:287
  180.2 212.0 %copy-start.10 = (f32[256]{0:T(256)S(1)}, f32[256]{0:T(256)}, u32[]{:S(2)}) copy-start(f32[256]{0:T(256)} %param.6) | copy-start | bytes 3076
  180.2 212.0 %copy-start.11 = (s32[256]{0:T(256)S(1)}, s32[256]{0:T(256)}, u32[]{:S(2)}) copy-start(s32[256]{0:T(256)} %param.8) | copy-start | bytes 3076
  180.2 213.6 %copy-start.9 = (f32[384]{0:T(512)S(1)}, f32[384]{0:T(512)}, u32[]{:S(2)}) copy-start(f32[384]{0:T(512)} %param.7) | copy-start | bytes 4612
  180.2 29.2 %collective-permute-start.5 = (f32[4,192,384]{2,1,0:T(8,128)S(1)}, f32[4,192,384]{2,1,0:T(8,128)S(1)}, u32[]{:S(2)}, u32[]{:S(2)}) collective-permute-start(f32[4,192,384]{2,1,0:T(8,128)S(1)} %dynamic-slice_bitcast_fusion), channel_id=1, source_target_pairs={{24,0},{0,8},{8,16},{16,24},{25,1},{1,9},{9,17},{17,25},{26,2},{2,... | collective-permute-start | bytes 3538952 | tf_op jit(solution)/shard_map/ppermute | solution.py:15
  181.4 30.1 %collective-permute-start.1 = (f32[8,192,384]{2,1,0:T(8,128)S(1)}, f32[8,192,384]{2,1,0:T(8,128)S(1)}, u32[]{:S(2)}, u32[]{:S(2)}) collective-permute-start(f32[8,192,384]{2,1,0:T(8,128)S(1)} %collective-permute-done.refs_0_), channel_id=1, source_target_pairs={{0,1},{1,0},{2,3},{3,2},{4,5},{5,4},{6,7},{7,6},{8,9},{9,8},{10,11... | collective-permute-start | bytes 7077896 | tf_op jit(solution)/shard_map/ppermute | solution.py:248
  181.4 200.7 %collective-permute-start.3 = (f32[8,192,384]{2,1,0:T(8,128)}, f32[8,192,384]{2,1,0:T(8,128)}, u32[]{:S(2)}, u32[]{:S(2)}) collective-permute-start(f32[8,192,384]{2,1,0:T(8,128)} %collective-permute-done.2.refs_2_), channel_id=1, source_target_pairs={{0,1},{1,0},{2,3},{3,2},{4,5},{5,4},{6,7},{7,6},{8,9},{9,8},{10,11... | collective-permute-start | bytes 7077896 | tf_op jit(solution)/shard_map/ppermute | solution.py:248
  209.4 172.7 %copy-start.3 = (f32[4,192,384]{2,1,0:T(8,128)}, f32[4,192,384]{2,1,0:T(8,128)S(1)}, u32[]{:S(2)}) copy-start(f32[4,192,384]{2,1,0:T(8,128)S(1)} %collective-permute-done.5.refs_8_) | copy-start | bytes 3538948
  209.4 147.7 %collective-permute-start.10 = (f32[4,192,384]{2,1,0:T(8,128)S(1)}, f32[4,192,384]{2,1,0:T(8,128)S(1)}, u32[]{:S(2)}, u32[]{:S(2)}) collective-permute-start(f32[4,192,384]{2,1,0:T(8,128)S(1)} %collective-permute-done.5.refs_8_), channel_id=1, source_target_pairs={{0,2},{1,3},{2,0},{3,1},{4,6},{5,7},{6,4},{7,5},{8,10},{9,11},{10,... | collective-permute-start | bytes 3538952 | tf_op jit(solution)/shard_map/ppermute | solution.py:248
  211.1 171.0 %collective-permute-start.7 = (f32[4,192,384]{2,1,0:T(8,128)S(1)}, f32[4,192,384]{2,1,0:T(8,128)S(1)}, u32[]{:S(2)}, u32[]{:S(2)}) collective-permute-start(f32[4,192,384]{2,1,0:T(8,128)S(1)} %collective-permute-done.4.refs_4_), channel_id=1, source_target_pairs={{0,2},{1,3},{2,0},{3,1},{4,6},{5,7},{6,4},{7,5},{8,10},{9,11},{10,... | collective-permute-start | bytes 3538952 | tf_op jit(solution)/shard_map/ppermute | solution.py:248
  211.5 170.7 %collective-permute-start.6 = (f32[4,192,384]{2,1,0:T(8,128)S(1)}, f32[4,192,384]{2,1,0:T(8,128)S(1)}, u32[]{:S(2)}, u32[]{:S(2)}) collective-permute-start(f32[4,192,384]{2,1,0:T(8,128)S(1)} %collective-permute-done.4.refs_4_), channel_id=1, source_target_pairs={{0,1},{1,0},{2,3},{3,2},{4,5},{5,4},{6,7},{7,6},{8,9},{9,8},{10,11... | collective-permute-start | bytes 3538952 | tf_op jit(solution)/shard_map/ppermute | solution.py:248
  211.5 1.4 copy-start.1
  212.9 169.3 %collective-permute-start.9 = (f32[4,192,384]{2,1,0:T(8,128)S(1)}, f32[4,192,384]{2,1,0:T(8,128)S(1)}, u32[]{:S(2)}, u32[]{:S(2)}) collective-permute-start(f32[4,192,384]{2,1,0:T(8,128)S(1)} %collective-permute-done.5.refs_8_), channel_id=1, source_target_pairs={{0,1},{1,0},{2,3},{3,2},{4,5},{5,4},{6,7},{7,6},{8,9},{9,8},{10,11... | collective-permute-start | bytes 3538952 | tf_op jit(solution)/shard_map/ppermute | solution.py:248
  357.1 25.1 %copy-start.4 = (f32[4,192,384]{2,1,0:T(8,128)}, f32[4,192,384]{2,1,0:T(8,128)S(1)}, u32[]{:S(2)}) copy-start(f32[4,192,384]{2,1,0:T(8,128)S(1)} %collective-permute-done.10.refs_10_) | copy-start | bytes 3538948
  357.1 25.1 %collective-permute-start.11 = (f32[4,192,384]{2,1,0:T(8,128)S(1)}, f32[4,192,384]{2,1,0:T(8,128)S(1)}, u32[]{:S(2)}, u32[]{:S(2)}) collective-permute-start(f32[4,192,384]{2,1,0:T(8,128)S(1)} %collective-permute-done.10.refs_10_), channel_id=1, source_target_pairs={{0,1},{1,0},{2,3},{3,2},{4,5},{5,4},{6,7},{7,6},{8,9},{9,8},{10,11... | collective-permute-start | bytes 3538952 | tf_op jit(solution)/shard_map/ppermute | solution.py:248
  382.1 1.4 copy-start.5
  382.1 3.0 collective-permute-start.8
  382.1 12.6 %copy-start.7 = (f32[4,192,384]{2,1,0:T(8,128)}, f32[4,192,384]{2,1,0:T(8,128)S(1)}, u32[]{:S(2)}) copy-start(f32[4,192,384]{2,1,0:T(8,128)S(1)} %collective-permute-done.9.refs_9_) | copy-start | bytes 3538948
  382.2 1.3 copy-start.6
  383.5 1.7 copy-start.8
  385.2 111.5 %all-to-all-start.2 = ((f32[8,2,192,384]{3,2,1,0:T(8,128)}), f32[8,2,192,384]{3,2,1,0:T(8,128)}, u32[]{:S(2)}, u32[]{:S(2)}) async-start(f32[8,2,192,384]{3,2,1,0:T(8,128)} %pack.4), calls=%async_computation.2 | async-start | bytes 9437184 | tf_op jit(solution)/shard_map/all_to_all | solution.py:287
  496.7 111.9 %all-to-all-start.5 = ((f32[8,2,192,384]{3,2,1,0:T(8,128)}), f32[8,2,192,384]{3,2,1,0:T(8,128)}, u32[]{:S(2)}, u32[]{:S(2)}) async-start(f32[8,2,192,384]{3,2,1,0:T(8,128)} %block_density.5), calls=%async_computation.5 | async-start | bytes 9437184 | tf_op jit(solution)/shard_map/all_to_all | solution.py:336
  608.7 211.4 %all-to-all-start.4 = ((f32[8,4,192,384]{3,2,1,0:T(8,128)}), f32[8,4,192,384]{3,2,1,0:T(8,128)}, u32[]{:S(2)}, u32[]{:S(2)}) async-start(f32[8,4,192,384]{3,2,1,0:T(8,128)} %block_density.4), calls=%async_computation.4 | async-start | bytes 18874368 | tf_op jit(solution)/shard_map/all_to_all | solution.py:336
  820.1 109.8 %all-to-all-start.3 = ((f32[8,2,192,384]{3,2,1,0:T(8,128)}), f32[8,2,192,384]{3,2,1,0:T(8,128)}, u32[]{:S(2)}, u32[]{:S(2)}) async-start(f32[8,2,192,384]{3,2,1,0:T(8,128)} %block_density.3), calls=%async_computation.3 | async-start | bytes 9437184 | tf_op jit(solution)/shard_map/all_to_all | solution.py:336

commit v4 on v3

--- a/solution.py
+++ b/solution.py
@@ -123,56 +123,59 @@
     )(i_levels, j_levels, vir_pair, j_high, j_low, b_block)
 
 
-def pack_kernel(at_ref, in_ref, out_ref):
-    for t in range(in_ref.shape[1]):
-        out_ref[t, 0] = in_ref[:, t, :]
-
-
-def pack(integrals, places, width):
+def pack_kernel(_, __, in_ref, out_ref):
+    out_ref[:, 0] = jnp.swapaxes(in_ref[...], 0, 1)
+
+
+def block_of(m, which, owners):
+    group, start, n_blocks = which[0], which[1], which[2]
+    first = owners[jnp.maximum(group, 0)]
+    return lax.rem(jnp.where(group < 0, 0, first) + start + m, n_blocks)
+
+
+def pack(integrals, which, owners, n_i, width):
     rows, _, n_vir = integrals.shape
-    n_i = places.shape[0]
     cuts = 2 if rows % 16 == 0 else 1
     tile = rows // cuts
     return pl.pallas_call(
         pack_kernel,
         grid_spec=pltpu.PrefetchScalarGridSpec(
-            num_scalar_prefetch=1,
+            num_scalar_prefetch=2,
             grid=(n_i, cuts),
-            in_specs=[pl.BlockSpec((tile, width, n_vir), lambda m, r, at: (r, at[m], 0))],
-            out_specs=pl.BlockSpec((width, 1, tile, n_vir), lambda m, r, at: (0, m, r, 0)),
+            in_specs=[pl.BlockSpec((tile, width, n_vir), lambda m, r, *at: (r, block_of(m, *at), 0))],
+            out_specs=pl.BlockSpec((width, 1, tile, n_vir), lambda m, r, *at: (0, m, r, 0)),
         ),
         out_shape=jax.ShapeDtypeStruct((width, n_i, rows, n_vir), jnp.float32),
         compiler_params=pltpu.CompilerParams(vmem_limit_bytes=vmem_bytes),
         cost_estimate=pl.CostEstimate(
             flops=0, bytes_accessed=8 * width * n_i * rows * n_vir, transcendentals=0),
         name="pack",
-    )(places, integrals)
-
-
-def place_kernel(at_ref, part_ref, *refs):
+    )(which, owners, integrals)
+
+
+def place_kernel(_, __, part_ref, *refs):
     out_ref = refs[-1]
-    for t in range(part_ref.shape[0]):
-        out_ref[:, t, :] = part_ref[t, 0]
-
-
-def place(part, places, out, shape):
+    out_ref[...] = jnp.swapaxes(part_ref[:, 0], 0, 1)
+
+
+def place(part, which, owners, out, shape):
     width, n_i, rows, n_vir = part.shape
     cuts = 2 if rows % 16 == 0 else 1
     tile = rows // cuts
-    operands = [places, part]
-    in_specs = [pl.BlockSpec((width, 1, tile, n_vir), lambda m, r, at: (0, m, r, 0))]
+    operands = [which, owners, part]
+    in_specs = [pl.BlockSpec((width, 1, tile, n_vir), lambda m, r, *at: (0, m, r, 0))]
     aliases = {}
     if out is not None:
         operands.append(out)
         in_specs.append(pl.BlockSpec(memory_space=pl.ANY))
-        aliases = {2: 0}
+        aliases = {3: 0}
     return pl.pallas_call(
         place_kernel,
         grid_spec=pltpu.PrefetchScalarGridSpec(
-            num_scalar_prefetch=1,
+            num_scalar_prefetch=2,
             grid=(n_i, cuts),
             in_specs=in_specs,
-            out_specs=pl.BlockSpec((tile, width, n_vir), lambda m, r, at: (r, at[m], 0)),
+            out_specs=pl.BlockSpec((tile, width, n_vir), lambda m, r, *at: (r, block_of(m, *at), 0)),
         ),
         out_shape=jax.ShapeDtypeStruct(shape, jnp.float32),
         input_output_aliases=aliases,
@@ -281,12 +284,14 @@
     places = (first + jnp.arange(n_blocks, dtype=jnp.int32)) % n_blocks
     n_i = 2 if n_blocks % 2 == 0 else 1
     ends = [0, n_i, n_blocks - n_i, n_blocks] if n_blocks >= 3 * n_i else [0, n_blocks]
-    chunks = [places[start:end] for start, end in zip(ends, ends[1:])]
+    planned = next_group if shared else jnp.int32(-1)
+    chunks = [(jnp.stack([planned, jnp.int32(start), jnp.int32(n_blocks)]), owners[0], end - start)
+              for start, end in zip(ends, ends[1:])]
 
     def send_in(part):
         return lax.all_to_all(part, "aux", split_axis=0, concat_axis=0, tiled=True)
 
-    parts = [pack(integrals, chunk, n_shards) for chunk in chunks]
+    parts = [pack(integrals, *chunk, n_shards) for chunk in chunks]
     blocks = [send_in(parts[0])]
     sent = lax.dynamic_slice_in_dim(integrals, next_owner * occ_block, occ_block, 1)
     arrived = from_behind(jnp.transpose(sent, (1, 0, 2)), "grp", 1)
@@ -313,7 +318,7 @@
         crossed = lax.optimization_barrier((crossed, late_own))[0]
         cross = within_half(crossed, n_half)
         late = within_half(late_own, n_half)
-        send_after(2, *near, *cross, *late)
+        send_after(2, late[n_half // 2], cross[n_half // 2])
         order = jnp.where(natural < n_half, far_start + natural, me ^ (natural - n_half))
         j_high, j_low = join_j(me, order, near, cross, late)
     else:
@@ -334,7 +339,7 @@
             i_levels[ends[c]:ends[c + 1]], j_levels, vir_pair, j_high, j_low, block)
         density = lax.optimization_barrier((density, blocks[-1]))[0]
         back = lax.all_to_all(density, "aux", split_axis=0, concat_axis=0, tiled=True)
-        out = place(back, chunk, out, integrals.shape)
+        out = place(back, *chunk[:2], out, integrals.shape)
     return out
 
 

time: 938 us -> 934 us (level)
    all_to_all x3, waiting for transfers between devices: 29.3 us -> 18.1 us  [send_in(): return lax.all_to_all(part, 'aux', split_axis=0, concat_axis=0, tiled=True)]
where the time goes in v4:
time: 934 us; the launch traced here: 932 us
  waiting for transfers between devices  594 us (64%)
  Pallas kernels  281 us (30%)
  starting transfers between devices  41.3 us (4%)
  local copies, waits for them, and re-layouts  10 us (1%)
    ppermute x10, waiting for transfers between devices, across(): return lax.ppermute(block, 'aux', route)  274 us
    all_to_all x3, waiting for transfers between devices, body(): lax.all_to_all(density, 'aux', split_axis=0, concat_axis=0, tiled=True)  239 us
    pallas_call x3, Pallas kernels, block_density(): pl.pallas_call(density_kernel, grid=(n_i // at_once, steps), in_specs=[sm...  219 us
    ppermute x2, waiting for transfers between devices, from_behind(): return lax.ppermute(block, axis, route)  63.9 us
    pallas_call x3, Pallas kernels, place(): pl.pallas_call(place_kernel, grid_spec=pltpu.PrefetchScalarGridSpec(num_s...  22.6 us
    pallas_call x3, Pallas kernels, pack(): pl.pallas_call(pack_kernel, grid_spec=pltpu.PrefetchScalarGridSpec(num_sc...  22.5 us
  transfers between devices with their start and end apart: 18, of which 11 were waited for; matrix products, arithmetic and copies ran while one was open for 1% of the time, Pallas kernels for 29%

profile of v4, /device:TPU:0, one launch (start us, length us, event | category | flops | bytes accessed | tf_op | source)
XLA Modules:
  0.0 932.3 jit_solution(18235900489694815376)
XLA Ops:
  0.0 0.6 pad_add_fusion._
  0.6 5.9 pack.5
  6.5 6.5 all-to-all-start
  13.0 0.7 constant_dynamic-slice_fusion.3
  14.3 1.8 constant_dynamic-slice_fusion.1
  16.1 0.5 copy.12
  16.6 1.5 collective-permute-start
  18.1 0.6 pad_add_fusion.1
  18.7 6.0 pack.4
  24.7 10.7 %pack.3 = f32[8,4,192,384]{3,2,1,0:T(8,128)} custom-call(s32[3]{0:T(128)} %get-tuple-element.35._, s32[4]{0:T(128)} %bitcast.13, f32[192,64,384]{2,1,0:T(8,128)} %in_ref.5), custom_call_target="tpu_custom_call" | custom-call | bytes 18874368 | tf_op jit(solution)/shard_map/pack/pallas_call | solution.py:140
  35.4 35.8 %collective-permute-done.refs_0_ = f32[8,192,384]{2,1,0:T(8,128)S(1)} collective-permute-done((f32[8,192,384]{2,1,0:T(8,128)S(1)}, f32[8,192,384]{2,1,0:T(8,128)S(1)}, u32[]{:S(2)}, u32[]{:S(2)}) %collective-permute-start) | collective-permute-done | bytes 2359328 | tf_op jit(solution)/shard_map/ppermute | solution.py:15
  71.2 1.7 collective-permute-start.2
  72.9 2.4 collective-permute-start.4
  75.3 90.4 %collective-permute-done.4.refs_4_ = f32[4,192,384]{2,1,0:T(8,128)S(1)} collective-permute-done((f32[4,192,384]{2,1,0:T(8,128)S(1)}, f32[4,192,384]{2,1,0:T(8,128)S(1)}, u32[]{:S(2)}, u32[]{:S(2)}) %collective-permute-start.4) | collective-permute-done | bytes 1179680 | tf_op jit(solution)/shard_map/ppermute | solution.py:251
  165.8 6.0 collective-permute-done.2.refs_2_
  171.8 5.0 all-to-all-start.1
  176.9 1.4 dynamic-slice_bitcast_fusion
  178.3 1.1 collective-permute-start.5
  179.4 28.1 %collective-permute-done.5.refs_8_ = f32[4,192,384]{2,1,0:T(8,128)S(1)} collective-permute-done((f32[4,192,384]{2,1,0:T(8,128)S(1)}, f32[4,192,384]{2,1,0:T(8,128)S(1)}, u32[]{:S(2)}, u32[]{:S(2)}) %collective-permute-start.5) | collective-permute-done | bytes 1179680 | tf_op jit(solution)/shard_map/ppermute | solution.py:15
  207.5 1.0 copy-done.3
  208.5 1.7 collective-permute-start.10
  210.5 144.6 %collective-permute-done.10.refs_10_ = f32[4,192,384]{2,1,0:T(8,128)S(1)} collective-permute-done((f32[4,192,384]{2,1,0:T(8,128)S(1)}, f32[4,192,384]{2,1,0:T(8,128)S(1)}, u32[]{:S(2)}, u32[]{:S(2)}) %collective-permute-start.10) | collective-permute-done | bytes 1179680 | tf_op jit(solution)/shard_map/ppermute | solution.py:251
  355.1 1.0 copy-done.4
  356.2 24.0 %collective-permute-done.7.refs_6_ = f32[4,192,384]{2,1,0:T(8,128)} collective-permute-done((f32[4,192,384]{2,1,0:T(8,128)S(1)}, f32[4,192,384]{2,1,0:T(8,128)}, u32[]{:S(2)}, u32[]{:S(2)}) %collective-permute-start.7) | collective-permute-done | bytes 1179680 | tf_op jit(solution)/shard_map/ppermute | solution.py:251
  380.2 3.1 all-to-all-done.1.b_ref
  383.2 4.8 all-to-all-start.2
  389.3 8.8 collective-permute-done.1.refs_1_
  398.1 1.4 copy-done.1
  400.5 0.6 fusion.2
  401.2 0.6 pad_add_fusion.3.at_ref
  402.0 0.7 select_reduce_fusion.1
  402.7 0.6 fusion.4
  403.3 1.0 add_add_fusion.vir_ref
  404.3 1.0 copy-done.5
  405.3 16.6 %join_j.1 = (bf16[4,1536,768]{2,1,0:T(8,128)(2,1)}, bf16[4,1536,768]{2,1,0:T(8,128)(2,1)}) custom-call(s32[9]{0:T(128)} %pad_add_fusion.3.at_ref, f32[8,192,384]{2,1,0:T(8,128)} %copy-done, f32[8,192,384]{2,1,0:T(8,128)} %copy-done.1, f32[8,192,384]{2,1,0:T(8,128)} %collective-permute-done.2.refs_2_, f32[8,192,384]{2,1,0:T(8,128)} %collective-permute-done.3.refs_3_, ...), custom_call_target="tpu_custom_call" | custom-call | bytes 37748736 | tf_op jit(solution)/shard_map/join_j/pallas_call | solution.py:233
  421.9 56.1 %block_density.5 = f32[8,2,192,384]{3,2,1,0:T(8,128)} custom-call(f32[2]{0:T(128)} %get-tuple-element.31.i_levels, f32[8]{0:T(128)} %get-tuple-element.27.j_levels, f32[384,384]{1,0:T(8,128)} %add_add_fusion.vir_ref, bf16[4,1536,768]{2,1,0:T(8,128)(2,1)} %get-tuple-element.18.high_ref, bf16[4,1536,768]{2,1,0:T(8,128)(2,1)} %get-tuple-element.19.low_ref, ...), custom_call_target="tpu_custom_call" | custom-call | flops 43486543872 | bytes 28311552 | tf_op jit(solution)/shard_map/block_density/pallas_call | solution.py:106
  478.0 15.1 %all-to-all-done.2.b_ref = f32[8,2,192,384]{3,2,1,0:T(8,128)} async-done(((f32[8,2,192,384]{3,2,1,0:T(8,128)}), f32[8,2,192,384]{3,2,1,0:T(8,128)}, u32[]{:S(2)}, u32[]{:S(2)}) %all-to-all-start.2) | async-done | bytes 4718624 | tf_op jit(solution)/shard_map/all_to_all | solution.py:292
  493.1 4.8 all-to-all-start.5
  497.9 0.6 slice.10.i_levels
  498.5 106.6 %block_density.4 = f32[8,4,192,384]{3,2,1,0:T(8,128)} custom-call(f32[4]{0:T(128)} %slice.10.i_levels, f32[8]{0:T(128)} %get-tuple-element.27.j_levels, f32[384,384]{1,0:T(8,128)} %add_add_fusion.vir_ref, bf16[4,1536,768]{2,1,0:T(8,128)(2,1)} %get-tuple-element.18.high_ref, bf16[4,1536,768]{2,1,0:T(8,128)(2,1)} %get-tuple-element.19.low_ref, ...), custom_call_target="tpu_custom_call" | custom-call | flops 86973087744 | bytes 37748736 | tf_op jit(solution)/shard_map/block_density/pallas_call | solution.py:106
  605.1 5.3 all-to-all-start.4
  610.4 56.1 %block_density.3 = f32[8,2,192,384]{3,2,1,0:T(8,128)} custom-call(f32[2]{0:T(128)} %get-tuple-element.32.i_levels, f32[8]{0:T(128)} %get-tuple-element.27.j_levels, f32[384,384]{1,0:T(8,128)} %add_add_fusion.vir_ref, bf16[4,1536,768]{2,1,0:T(8,128)(2,1)} %get-tuple-element.18.high_ref, bf16[4,1536,768]{2,1,0:T(8,128)(2,1)} %get-tuple-element.19.low_ref, ...), custom_call_target="tpu_custom_call" | custom-call | flops 43486543872 | bytes 28311552 | tf_op jit(solution)/shard_map/block_density/pallas_call | solution.py:106
  666.5 150.0 %all-to-all-done.4.part_ref = f32[8,4,192,384]{3,2,1,0:T(8,128)} async-done(((f32[8,4,192,384]{3,2,1,0:T(8,128)}), f32[8,4,192,384]{3,2,1,0:T(8,128)}, u32[]{:S(2)}, u32[]{:S(2)}) %all-to-all-start.4) | async-done | bytes 9437216 | tf_op jit(solution)/shard_map/all_to_all | solution.py:341
  816.5 4.6 all-to-all-start.3
  821.1 6.0 place.3.refs_0_
  827.0 10.7 %place.4.refs_0_ = f32[192,64,384]{2,1,0:T(8,128)} custom-call(s32[3]{0:T(128)} %get-tuple-element.35._, s32[4]{0:T(128)} %bitcast.15, f32[8,4,192,384]{3,2,1,0:T(8,128)} %all-to-all-done.4.part_ref, f32[192,64,384]{2,1,0:T(8,128)} %place.3.refs_0_), custom_call_target="tpu_custom_call", output_to_operand_aliasing={{}: (3, {})} | custom-call | bytes 18874368 | tf_op jit(solution)/shard_map/place/pallas_call | solution.py:172
  837.8 88.6 %all-to-all-done.3.part_ref = f32[8,2,192,384]{3,2,1,0:T(8,128)} async-done(((f32[8,2,192,384]{3,2,1,0:T(8,128)}), f32[8,2,192,384]{3,2,1,0:T(8,128)}, u32[]{:S(2)}, u32[]{:S(2)}) %all-to-all-start.3) | async-done | bytes 4718624 | tf_op jit(solution)/shard_map/all_to_all | solution.py:341
  926.3 6.0 place.5
  (33 shorter events, 2.3 us)
Async XLA Ops:
  6.5 6.5 copy-start.6
  6.5 165.3 %all-to-all-start = ((f32[8,2,192,384]{3,2,1,0:T(8,128)}), f32[8,2,192,384]{3,2,1,0:T(8,128)}, u32[]{:S(2)}, u32[]{:S(2)}) async-start(f32[8,2,192,384]{3,2,1,0:T(8,128)} %pack.5), calls=%async_computation | async-start | bytes 9437184 | tf_op jit(solution)/shard_map/all_to_all | solution.py:292
  16.6 54.6 %collective-permute-start = (f32[8,192,384]{2,1,0:T(8,128)S(1)}, f32[8,192,384]{2,1,0:T(8,128)S(1)}, u32[]{:S(2)}, u32[]{:S(2)}) collective-permute-start(f32[8,192,384]{2,1,0:T(8,128)S(1)} %bitcast.10), channel_id=1, source_target_pairs={{24,0},{0,8},{8,16},{16,24},{25,1},{1,9},{9,17},{17,25},{26,2},{2,... | collective-permute-start | bytes 7077896 | tf_op jit(solution)/shard_map/ppermute | solution.py:15
  71.2 316.9 %copy-start = (f32[8,192,384]{2,1,0:T(8,128)}, f32[8,192,384]{2,1,0:T(8,128)S(1)}, u32[]{:S(2)}) copy-start(f32[8,192,384]{2,1,0:T(8,128)S(1)} %collective-permute-done.refs_0_) | copy-start | bytes 7077892
  71.2 100.7 %collective-permute-start.2 = (f32[8,192,384]{2,1,0:T(8,128)S(1)}, f32[8,192,384]{2,1,0:T(8,128)}, u32[]{:S(2)}, u32[]{:S(2)}) collective-permute-start(f32[8,192,384]{2,1,0:T(8,128)S(1)} %collective-permute-done.refs_0_), channel_id=1, source_target_pairs={{0,2},{1,3},{2,0},{3,1},{4,6},{5,7},{6,4},{7,5},{8,10},{9,11},{10,... | collective-permute-start | bytes 7077896 | tf_op jit(solution)/shard_map/ppermute | solution.py:251
  72.9 92.9 %collective-permute-start.4 = (f32[4,192,384]{2,1,0:T(8,128)S(1)}, f32[4,192,384]{2,1,0:T(8,128)S(1)}, u32[]{:S(2)}, u32[]{:S(2)}) collective-permute-start(f32[4,192,384]{2,1,0:T(8,128)S(1)} %constant_dynamic-slice_fusion), channel_id=1, source_target_pairs={{0,4},{1,5},{2,6},{3,7},{4,0},{5,1},{6,2},{7,3},{8,12},{9,13},{10,... | collective-permute-start | bytes 3538952 | tf_op jit(solution)/shard_map/ppermute | solution.py:251
  165.8 222.8 %copy-start.2 = (f32[4,192,384]{2,1,0:T(8,128)}, f32[4,192,384]{2,1,0:T(8,128)S(1)}, u32[]{:S(2)}) copy-start(f32[4,192,384]{2,1,0:T(8,128)S(1)} %collective-permute-done.4.refs_4_) | copy-start | bytes 3538948
  171.8 211.4 %all-to-all-start.1 = ((f32[8,4,192,384]{3,2,1,0:T(8,128)}), f32[8,4,192,384]{3,2,1,0:T(8,128)}, u32[]{:S(2)}, u32[]{:S(2)}) async-start(f32[8,4,192,384]{3,2,1,0:T(8,128)} %pack.3), calls=%async_computation.1 | async-start | bytes 18874368 | tf_op jit(solution)/shard_map/all_to_all | solution.py:292
  178.3 223.6 %copy-start.8 = (f32[256]{0:T(256)S(1)}, f32[256]{0:T(256)}, u32[]{:S(2)}) copy-start(f32[256]{0:T(256)} %param.6) | copy-start | bytes 3076
  178.3 223.6 %copy-start.9 = (s32[256]{0:T(256)S(1)}, s32[256]{0:T(256)}, u32[]{:S(2)}) copy-start(s32[256]{0:T(256)} %param.8) | copy-start | bytes 3076
  178.3 225.0 %copy-start.7 = (f32[384]{0:T(512)S(1)}, f32[384]{0:T(512)}, u32[]{:S(2)}) copy-start(f32[384]{0:T(512)} %param.7) | copy-start | bytes 4612
  178.3 29.2 %collective-permute-start.5 = (f32[4,192,384]{2,1,0:T(8,128)S(1)}, f32[4,192,384]{2,1,0:T(8,128)S(1)}, u32[]{:S(2)}, u32[]{:S(2)}) collective-permute-start(f32[4,192,384]{2,1,0:T(8,128)S(1)} %dynamic-slice_bitcast_fusion), channel_id=1, source_target_pairs={{24,0},{0,8},{8,16},{16,24},{25,1},{1,9},{9,17},{17,25},{26,2},{2,... | collective-permute-start | bytes 3538952 | tf_op jit(solution)/shard_map/ppermute | solution.py:15
  207.5 1.0 copy-start.3
  208.5 146.6 %collective-permute-start.10 = (f32[4,192,384]{2,1,0:T(8,128)S(1)}, f32[4,192,384]{2,1,0:T(8,128)S(1)}, u32[]{:S(2)}, u32[]{:S(2)}) collective-permute-start(f32[4,192,384]{2,1,0:T(8,128)S(1)} %collective-permute-done.5.refs_8_), channel_id=1, source_target_pairs={{0,2},{1,3},{2,0},{3,1},{4,6},{5,7},{6,4},{7,5},{8,10},{9,11},{10,... | collective-permute-start | bytes 3538952 | tf_op jit(solution)/shard_map/ppermute | solution.py:251
  210.2 170.0 %collective-permute-start.7 = (f32[4,192,384]{2,1,0:T(8,128)S(1)}, f32[4,192,384]{2,1,0:T(8,128)}, u32[]{:S(2)}, u32[]{:S(2)}) collective-permute-start(f32[4,192,384]{2,1,0:T(8,128)S(1)} %collective-permute-done.4.refs_4_), channel_id=1, source_target_pairs={{0,2},{1,3},{2,0},{3,1},{4,6},{5,7},{6,4},{7,5},{8,10},{9,11},{10,... | collective-permute-start | bytes 3538952 | tf_op jit(solution)/shard_map/ppermute | solution.py:251
  355.1 1.0 copy-start.4
  383.2 109.8 %all-to-all-start.2 = ((f32[8,2,192,384]{3,2,1,0:T(8,128)}), f32[8,2,192,384]{3,2,1,0:T(8,128)}, u32[]{:S(2)}, u32[]{:S(2)}) async-start(f32[8,2,192,384]{3,2,1,0:T(8,128)} %pack.4), calls=%async_computation.2 | async-start | bytes 9437184 | tf_op jit(solution)/shard_map/all_to_all | solution.py:292
  388.0 10.0 %collective-permute-start.1 = (f32[8,192,384]{2,1,0:T(8,128)S(1)}, f32[8,192,384]{2,1,0:T(8,128)S(1)}, u32[]{:S(2)}, u32[]{:S(2)}) collective-permute-start(f32[8,192,384]{2,1,0:T(8,128)S(1)} %collective-permute-done.refs_0_), channel_id=1, source_target_pairs={{0,1},{1,0},{2,3},{3,2},{4,5},{5,4},{6,7},{7,6},{8,9},{9,8},{10,11... | collective-permute-start | bytes 7077896 | tf_op jit(solution)/shard_map/ppermute | solution.py:251
  388.2 16.0 %collective-permute-start.3 = (f32[8,192,384]{2,1,0:T(8,128)}, f32[8,192,384]{2,1,0:T(8,128)}, u32[]{:S(2)}, u32[]{:S(2)}) collective-permute-start(f32[8,192,384]{2,1,0:T(8,128)} %collective-permute-done.2.refs_2_), channel_id=1, source_target_pairs={{0,1},{1,0},{2,3},{3,2},{4,5},{5,4},{6,7},{7,6},{8,9},{9,8},{10,11... | collective-permute-start | bytes 7077896 | tf_op jit(solution)/shard_map/ppermute | solution.py:251
  388.6 15.6 %collective-permute-start.6 = (f32[4,192,384]{2,1,0:T(8,128)S(1)}, f32[4,192,384]{2,1,0:T(8,128)}, u32[]{:S(2)}, u32[]{:S(2)}) collective-permute-start(f32[4,192,384]{2,1,0:T(8,128)S(1)} %collective-permute-done.4.refs_4_), channel_id=1, source_target_pairs={{0,1},{1,0},{2,3},{3,2},{4,5},{5,4},{6,7},{7,6},{8,9},{9,8},{10,11... | collective-permute-start | bytes 3538952 | tf_op jit(solution)/shard_map/ppermute | solution.py:251
  388.7 15.5 %collective-permute-start.9 = (f32[4,192,384]{2,1,0:T(8,128)}, f32[4,192,384]{2,1,0:T(8,128)}, u32[]{:S(2)}, u32[]{:S(2)}) collective-permute-start(f32[4,192,384]{2,1,0:T(8,128)} %copy-done.3), channel_id=1, source_target_pairs={{0,1},{1,0},{2,3},{3,2},{4,5},{5,4},{6,7},{7,6},{8,9},{9,8},{10,11... | collective-permute-start | bytes 3538952 | tf_op jit(solution)/shard_map/ppermute | solution.py:251
  389.1 15.1 %collective-permute-start.11 = (f32[4,192,384]{2,1,0:T(8,128)}, f32[4,192,384]{2,1,0:T(8,128)}, u32[]{:S(2)}, u32[]{:S(2)}) collective-permute-start(f32[4,192,384]{2,1,0:T(8,128)} %copy-done.4), channel_id=1, source_target_pairs={{0,1},{1,0},{2,3},{3,2},{4,5},{5,4},{6,7},{7,6},{8,9},{9,8},{10,11... | collective-permute-start | bytes 3538952 | tf_op jit(solution)/shard_map/ppermute | solution.py:251
  398.1 1.4 copy-start.1
  399.5 4.8 collective-permute-start.8
  404.3 1.0 copy-start.5
  493.1 112.0 %all-to-all-start.5 = ((f32[8,2,192,384]{3,2,1,0:T(8,128)}), f32[8,2,192,384]{3,2,1,0:T(8,128)}, u32[]{:S(2)}, u32[]{:S(2)}) async-start(f32[8,2,192,384]{3,2,1,0:T(8,128)} %block_density.5), calls=%async_computation.5 | async-start | bytes 9437184 | tf_op jit(solution)/shard_map/all_to_all | solution.py:341
  605.1 211.4 %all-to-all-start.4 = ((f32[8,4,192,384]{3,2,1,0:T(8,128)}), f32[8,4,192,384]{3,2,1,0:T(8,128)}, u32[]{:S(2)}, u32[]{:S(2)}) async-start(f32[8,4,192,384]{3,2,1,0:T(8,128)} %block_density.4), calls=%async_computation.4 | async-start | bytes 18874368 | tf_op jit(solution)/shard_map/all_to_all | solution.py:341
  816.5 109.8 %all-to-all-start.3 = ((f32[8,2,192,384]{3,2,1,0:T(8,128)}), f32[8,2,192,384]{3,2,1,0:T(8,128)}, u32[]{:S(2)}, u32[]{:S(2)}) async-start(f32[8,2,192,384]{3,2,1,0:T(8,128)} %block_density.3), calls=%async_computation.3 | async-start | bytes 9437184 | tf_op jit(solution)/shard_map/all_to_all | solution.py:341

commit v5 on v4

--- a/solution.py
+++ b/solution.py
@@ -85,13 +85,15 @@
             amp_high[at] = high
             amp_low[at] = low
 
-    @pl.loop(0, shards // merge)
+    group = merge * (2 if (shards // merge) % 2 == 0 else 1)
+
+    @pl.loop(0, shards // group)
     def _(s):
-        at = pl.ds(pl.multiple_of(s * (merge * rows), merge * rows), merge * rows)
+        at = pl.ds(pl.multiple_of(s * (group * rows), group * rows), group * rows)
         part = dot3(high_ref[0, at, :], low_ref[0, at, :], amp_high[...], amp_low[...])
-        for m in range(merge):
+        for m in range(group):
             for i in range(n_i):
-                out_ref[s * merge + m, i] += part[m * rows:(m + 1) * rows, i * n_vir:(i + 1) * n_vir]
+                out_ref[s * group + m, i] += part[m * rows:(m + 1) * rows, i * n_vir:(i + 1) * n_vir]
 
 
 def block_density(i_levels, j_levels, vir_pair, j_high, j_low, b_block):

time: 934 us -> 932 us (level)
  transfers between devices with their start and end apart: 18 -> 18, of which waited for: 11 -> 12; matrix products, arithmetic and copies ran while one was open for 1% -> 1% of each run, Pallas kernels for 29% -> 28%
where the time goes in v5:
time: 932 us; the launch traced here: 930 us
  waiting for transfers between devices  598 us (64%)
  Pallas kernels  275 us (30%)
  starting transfers between devices  41.3 us (4%)
  local copies, waits for them, and re-layouts  10 us (1%)
    ppermute x10, waiting for transfers between devices, across(): return lax.ppermute(block, 'aux', route)  274 us
    all_to_all x3, waiting for transfers between devices, body(): lax.all_to_all(density, 'aux', split_axis=0, concat_axis=0, tiled=True)  241 us
    pallas_call x3, Pallas kernels, block_density(): pl.pallas_call(density_kernel, grid=(n_i // at_once, steps), in_specs=[sm...  213 us
    ppermute x2, waiting for transfers between devices, from_behind(): return lax.ppermute(block, axis, route)  63.9 us
    pallas_call x3, Pallas kernels, place(): pl.pallas_call(place_kernel, grid_spec=pltpu.PrefetchScalarGridSpec(num_s...  22.6 us
    pallas_call x3, Pallas kernels, pack(): pl.pallas_call(pack_kernel, grid_spec=pltpu.PrefetchScalarGridSpec(num_sc...  22.5 us
    all_to_all x3, waiting for transfers between devices, send_in(): return lax.all_to_all(part, 'aux', split_axis=0, concat_axis=0, tiled=True)  19.5 us
  transfers between devices with their start and end apart: 18, of which 12 were waited for; matrix products, arithmetic and copies ran while one was open for 1% of the time, Pallas kernels for 28%

profile of v5, /device:TPU:0, one launch (start us, length us, event | category | flops | bytes accessed | tf_op | source)
XLA Modules:
  0.0 930.2 jit_solution(11839612547401243631)
XLA Ops:
  0.0 0.6 pad_add_fusion._
  0.6 5.9 pack.5
  6.5 6.5 all-to-all-start
  13.0 0.7 constant_dynamic-slice_fusion.3
  14.3 1.8 constant_dynamic-slice_fusion.1
  16.6 1.5 collective-permute-start
  18.1 0.6 pad_add_fusion.1
  18.7 6.0 pack.4
  24.7 10.7 %pack.3 = f32[8,4,192,384]{3,2,1,0:T(8,128)} custom-call(s32[3]{0:T(128)} %get-tuple-element.35._, s32[4]{0:T(128)} %bitcast.13, f32[192,64,384]{2,1,0:T(8,128)} %in_ref.5), custom_call_target="tpu_custom_call" | custom-call | bytes 18874368 | tf_op jit(solution)/shard_map/pack/pallas_call | solution.py:142
  35.4 35.8 %collective-permute-done.refs_0_ = f32[8,192,384]{2,1,0:T(8,128)S(1)} collective-permute-done((f32[8,192,384]{2,1,0:T(8,128)S(1)}, f32[8,192,384]{2,1,0:T(8,128)S(1)}, u32[]{:S(2)}, u32[]{:S(2)}) %collective-permute-start) | collective-permute-done | bytes 2359328 | tf_op jit(solution)/shard_map/ppermute | solution.py:15
  71.2 1.7 collective-permute-start.2
  72.9 2.4 collective-permute-start.4
  75.3 90.4 %collective-permute-done.4.refs_4_ = f32[4,192,384]{2,1,0:T(8,128)S(1)} collective-permute-done((f32[4,192,384]{2,1,0:T(8,128)S(1)}, f32[4,192,384]{2,1,0:T(8,128)S(1)}, u32[]{:S(2)}, u32[]{:S(2)}) %collective-permute-start.4) | collective-permute-done | bytes 1179680 | tf_op jit(solution)/shard_map/ppermute | solution.py:253
  165.8 6.0 collective-permute-done.2.refs_2_
  171.8 5.0 all-to-all-start.1
  176.9 1.4 dynamic-slice_bitcast_fusion
  178.3 1.1 collective-permute-start.5
  179.4 28.1 %collective-permute-done.5.refs_8_ = f32[4,192,384]{2,1,0:T(8,128)S(1)} collective-permute-done((f32[4,192,384]{2,1,0:T(8,128)S(1)}, f32[4,192,384]{2,1,0:T(8,128)S(1)}, u32[]{:S(2)}, u32[]{:S(2)}) %collective-permute-start.5) | collective-permute-done | bytes 1179680 | tf_op jit(solution)/shard_map/ppermute | solution.py:15
  207.5 1.0 copy-done.3
  208.5 1.7 collective-permute-start.10
  210.5 144.6 %collective-permute-done.10.refs_10_ = f32[4,192,384]{2,1,0:T(8,128)S(1)} collective-permute-done((f32[4,192,384]{2,1,0:T(8,128)S(1)}, f32[4,192,384]{2,1,0:T(8,128)S(1)}, u32[]{:S(2)}, u32[]{:S(2)}) %collective-permute-start.10) | collective-permute-done | bytes 1179680 | tf_op jit(solution)/shard_map/ppermute | solution.py:253
  355.1 1.0 copy-done.4
  356.2 24.0 %collective-permute-done.7.refs_6_ = f32[4,192,384]{2,1,0:T(8,128)} collective-permute-done((f32[4,192,384]{2,1,0:T(8,128)S(1)}, f32[4,192,384]{2,1,0:T(8,128)}, u32[]{:S(2)}, u32[]{:S(2)}) %collective-permute-start.7) | collective-permute-done | bytes 1179680 | tf_op jit(solution)/shard_map/ppermute | solution.py:253
  380.2 3.1 all-to-all-done.1.b_ref
  383.2 4.8 all-to-all-start.2
  389.3 8.8 collective-permute-done.1.refs_1_
  398.1 1.4 copy-done.1
  400.5 0.6 fusion.2
  401.2 0.6 pad_add_fusion.3.at_ref
  402.0 0.7 select_reduce_fusion.1
  402.7 0.6 fusion.4
  403.3 1.0 add_add_fusion.vir_ref
  404.3 1.0 copy-done.5
  405.3 16.6 %join_j.1 = (bf16[4,1536,768]{2,1,0:T(8,128)(2,1)}, bf16[4,1536,768]{2,1,0:T(8,128)(2,1)}) custom-call(s32[9]{0:T(128)} %pad_add_fusion.3.at_ref, f32[8,192,384]{2,1,0:T(8,128)} %copy-done, f32[8,192,384]{2,1,0:T(8,128)} %copy-done.1, f32[8,192,384]{2,1,0:T(8,128)} %collective-permute-done.2.refs_2_, f32[8,192,384]{2,1,0:T(8,128)} %collective-permute-done.3.refs_3_, ...), custom_call_target="tpu_custom_call" | custom-call | bytes 37748736 | tf_op jit(solution)/shard_map/join_j/pallas_call | solution.py:235
  421.9 54.7 %block_density.5 = f32[8,2,192,384]{3,2,1,0:T(8,128)} custom-call(f32[2]{0:T(128)} %get-tuple-element.31.i_levels, f32[8]{0:T(128)} %get-tuple-element.27.j_levels, f32[384,384]{1,0:T(8,128)} %add_add_fusion.vir_ref, bf16[4,1536,768]{2,1,0:T(8,128)(2,1)} %get-tuple-element.18.high_ref, bf16[4,1536,768]{2,1,0:T(8,128)(2,1)} %get-tuple-element.19.low_ref, ...), custom_call_target="tpu_custom_call" | custom-call | flops 43486543872 | bytes 28311552 | tf_op jit(solution)/shard_map/block_density/pallas_call | solution.py:108
  476.6 16.5 %all-to-all-done.2.b_ref = f32[8,2,192,384]{3,2,1,0:T(8,128)} async-done(((f32[8,2,192,384]{3,2,1,0:T(8,128)}), f32[8,2,192,384]{3,2,1,0:T(8,128)}, u32[]{:S(2)}, u32[]{:S(2)}) %all-to-all-start.2) | async-done | bytes 4718624 | tf_op jit(solution)/shard_map/all_to_all | solution.py:294
  493.1 4.8 all-to-all-start.5
  497.9 0.6 slice.10.i_levels
  498.5 103.8 %block_density.4 = f32[8,4,192,384]{3,2,1,0:T(8,128)} custom-call(f32[4]{0:T(128)} %slice.10.i_levels, f32[8]{0:T(128)} %get-tuple-element.27.j_levels, f32[384,384]{1,0:T(8,128)} %add_add_fusion.vir_ref, bf16[4,1536,768]{2,1,0:T(8,128)(2,1)} %get-tuple-element.18.high_ref, bf16[4,1536,768]{2,1,0:T(8,128)(2,1)} %get-tuple-element.19.low_ref, ...), custom_call_target="tpu_custom_call" | custom-call | flops 86973087744 | bytes 37748736 | tf_op jit(solution)/shard_map/block_density/pallas_call | solution.py:108
  602.3 0.7 all-to-all-done.5.part_ref
  602.9 5.3 all-to-all-start.4
  608.3 54.7 %block_density.3 = f32[8,2,192,384]{3,2,1,0:T(8,128)} custom-call(f32[2]{0:T(128)} %get-tuple-element.32.i_levels, f32[8]{0:T(128)} %get-tuple-element.27.j_levels, f32[384,384]{1,0:T(8,128)} %add_add_fusion.vir_ref, bf16[4,1536,768]{2,1,0:T(8,128)(2,1)} %get-tuple-element.18.high_ref, bf16[4,1536,768]{2,1,0:T(8,128)(2,1)} %get-tuple-element.19.low_ref, ...), custom_call_target="tpu_custom_call" | custom-call | flops 43486543872 | bytes 28311552 | tf_op jit(solution)/shard_map/block_density/pallas_call | solution.py:108
  663.0 151.4 %all-to-all-done.4.part_ref = f32[8,4,192,384]{3,2,1,0:T(8,128)} async-done(((f32[8,4,192,384]{3,2,1,0:T(8,128)}), f32[8,4,192,384]{3,2,1,0:T(8,128)}, u32[]{:S(2)}, u32[]{:S(2)}) %all-to-all-start.4) | async-done | bytes 9437216 | tf_op jit(solution)/shard_map/all_to_all | solution.py:343
  814.4 4.6 all-to-all-start.3
  819.0 6.0 place.3.refs_0_
  824.9 10.7 %place.4.refs_0_ = f32[192,64,384]{2,1,0:T(8,128)} custom-call(s32[3]{0:T(128)} %get-tuple-element.35._, s32[4]{0:T(128)} %bitcast.15, f32[8,4,192,384]{3,2,1,0:T(8,128)} %all-to-all-done.4.part_ref, f32[192,64,384]{2,1,0:T(8,128)} %place.3.refs_0_), custom_call_target="tpu_custom_call", output_to_operand_aliasing={{}: (3, {})} | custom-call | bytes 18874368 | tf_op jit(solution)/shard_map/place/pallas_call | solution.py:174
  835.6 88.6 %all-to-all-done.3.part_ref = f32[8,2,192,384]{3,2,1,0:T(8,128)} async-done(((f32[8,2,192,384]{3,2,1,0:T(8,128)}), f32[8,2,192,384]{3,2,1,0:T(8,128)}, u32[]{:S(2)}, u32[]{:S(2)}) %all-to-all-start.3) | async-done | bytes 4718624 | tf_op jit(solution)/shard_map/all_to_all | solution.py:343
  924.2 6.0 place.5
  (33 shorter events, 2.7 us)
Async XLA Ops:
  6.5 6.5 copy-start.6
  6.5 165.3 %all-to-all-start = ((f32[8,2,192,384]{3,2,1,0:T(8,128)}), f32[8,2,192,384]{3,2,1,0:T(8,128)}, u32[]{:S(2)}, u32[]{:S(2)}) async-start(f32[8,2,192,384]{3,2,1,0:T(8,128)} %pack.5), calls=%async_computation | async-start | bytes 9437184 | tf_op jit(solution)/shard_map/all_to_all | solution.py:294
  16.6 54.6 %collective-permute-start = (f32[8,192,384]{2,1,0:T(8,128)S(1)}, f32[8,192,384]{2,1,0:T(8,128)S(1)}, u32[]{:S(2)}, u32[]{:S(2)}) collective-permute-start(f32[8,192,384]{2,1,0:T(8,128)S(1)} %bitcast.10), channel_id=1, source_target_pairs={{24,0},{0,8},{8,16},{16,24},{25,1},{1,9},{9,17},{17,25},{26,2},{2,... | collective-permute-start | bytes 7077896 | tf_op jit(solution)/shard_map/ppermute | solution.py:15
  71.2 316.9 %copy-start = (f32[8,192,384]{2,1,0:T(8,128)}, f32[8,192,384]{2,1,0:T(8,128)S(1)}, u32[]{:S(2)}) copy-start(f32[8,192,384]{2,1,0:T(8,128)S(1)} %collective-permute-done.refs_0_) | copy-start | bytes 7077892
  71.2 100.7 %collective-permute-start.2 = (f32[8,192,384]{2,1,0:T(8,128)S(1)}, f32[8,192,384]{2,1,0:T(8,128)}, u32[]{:S(2)}, u32[]{:S(2)}) collective-permute-start(f32[8,192,384]{2,1,0:T(8,128)S(1)} %collective-permute-done.refs_0_), channel_id=1, source_target_pairs={{0,2},{1,3},{2,0},{3,1},{4,6},{5,7},{6,4},{7,5},{8,10},{9,11},{10,... | collective-permute-start | bytes 7077896 | tf_op jit(solution)/shard_map/ppermute | solution.py:253
  72.9 92.9 %collective-permute-start.4 = (f32[4,192,384]{2,1,0:T(8,128)S(1)}, f32[4,192,384]{2,1,0:T(8,128)S(1)}, u32[]{:S(2)}, u32[]{:S(2)}) collective-permute-start(f32[4,192,384]{2,1,0:T(8,128)S(1)} %constant_dynamic-slice_fusion), channel_id=1, source_target_pairs={{0,4},{1,5},{2,6},{3,7},{4,0},{5,1},{6,2},{7,3},{8,12},{9,13},{10,... | collective-permute-start | bytes 3538952 | tf_op jit(solution)/shard_map/ppermute | solution.py:253
  165.8 222.8 %copy-start.2 = (f32[4,192,384]{2,1,0:T(8,128)}, f32[4,192,384]{2,1,0:T(8,128)S(1)}, u32[]{:S(2)}) copy-start(f32[4,192,384]{2,1,0:T(8,128)S(1)} %collective-permute-done.4.refs_4_) | copy-start | bytes 3538948
  171.8 211.4 %all-to-all-start.1 = ((f32[8,4,192,384]{3,2,1,0:T(8,128)}), f32[8,4,192,384]{3,2,1,0:T(8,128)}, u32[]{:S(2)}, u32[]{:S(2)}) async-start(f32[8,4,192,384]{3,2,1,0:T(8,128)} %pack.3), calls=%async_computation.1 | async-start | bytes 18874368 | tf_op jit(solution)/shard_map/all_to_all | solution.py:294
  178.3 223.6 %copy-start.8 = (f32[256]{0:T(256)S(1)}, f32[256]{0:T(256)}, u32[]{:S(2)}) copy-start(f32[256]{0:T(256)} %param.6) | copy-start | bytes 3076
  178.3 223.6 %copy-start.9 = (s32[256]{0:T(256)S(1)}, s32[256]{0:T(256)}, u32[]{:S(2)}) copy-start(s32[256]{0:T(256)} %param.8) | copy-start | bytes 3076
  178.3 225.0 %copy-start.7 = (f32[384]{0:T(512)S(1)}, f32[384]{0:T(512)}, u32[]{:S(2)}) copy-start(f32[384]{0:T(512)} %param.7) | copy-start | bytes 4612
  178.3 29.2 %collective-permute-start.5 = (f32[4,192,384]{2,1,0:T(8,128)S(1)}, f32[4,192,384]{2,1,0:T(8,128)S(1)}, u32[]{:S(2)}, u32[]{:S(2)}) collective-permute-start(f32[4,192,384]{2,1,0:T(8,128)S(1)} %dynamic-slice_bitcast_fusion), channel_id=1, source_target_pairs={{24,0},{0,8},{8,16},{16,24},{25,1},{1,9},{9,17},{17,25},{26,2},{2,... | collective-permute-start | bytes 3538952 | tf_op jit(solution)/shard_map/ppermute | solution.py:15
  207.5 1.0 copy-start.3
  208.5 146.6 %collective-permute-start.10 = (f32[4,192,384]{2,1,0:T(8,128)S(1)}, f32[4,192,384]{2,1,0:T(8,128)S(1)}, u32[]{:S(2)}, u32[]{:S(2)}) collective-permute-start(f32[4,192,384]{2,1,0:T(8,128)S(1)} %collective-permute-done.5.refs_8_), channel_id=1, source_target_pairs={{0,2},{1,3},{2,0},{3,1},{4,6},{5,7},{6,4},{7,5},{8,10},{9,11},{10,... | collective-permute-start | bytes 3538952 | tf_op jit(solution)/shard_map/ppermute | solution.py:253
  210.2 170.0 %collective-permute-start.7 = (f32[4,192,384]{2,1,0:T(8,128)S(1)}, f32[4,192,384]{2,1,0:T(8,128)}, u32[]{:S(2)}, u32[]{:S(2)}) collective-permute-start(f32[4,192,384]{2,1,0:T(8,128)S(1)} %collective-permute-done.4.refs_4_), channel_id=1, source_target_pairs={{0,2},{1,3},{2,0},{3,1},{4,6},{5,7},{6,4},{7,5},{8,10},{9,11},{10,... | collective-permute-start | bytes 3538952 | tf_op jit(solution)/shard_map/ppermute | solution.py:253
  355.1 1.0 copy-start.4
  383.2 109.8 %all-to-all-start.2 = ((f32[8,2,192,384]{3,2,1,0:T(8,128)}), f32[8,2,192,384]{3,2,1,0:T(8,128)}, u32[]{:S(2)}, u32[]{:S(2)}) async-start(f32[8,2,192,384]{3,2,1,0:T(8,128)} %pack.4), calls=%async_computation.2 | async-start | bytes 9437184 | tf_op jit(solution)/shard_map/all_to_all | solution.py:294
  388.0 10.0 %collective-permute-start.1 = (f32[8,192,384]{2,1,0:T(8,128)S(1)}, f32[8,192,384]{2,1,0:T(8,128)S(1)}, u32[]{:S(2)}, u32[]{:S(2)}) collective-permute-start(f32[8,192,384]{2,1,0:T(8,128)S(1)} %collective-permute-done.refs_0_), channel_id=1, source_target_pairs={{0,1},{1,0},{2,3},{3,2},{4,5},{5,4},{6,7},{7,6},{8,9},{9,8},{10,11... | collective-permute-start | bytes 7077896 | tf_op jit(solution)/shard_map/ppermute | solution.py:253
  388.2 16.0 %collective-permute-start.3 = (f32[8,192,384]{2,1,0:T(8,128)}, f32[8,192,384]{2,1,0:T(8,128)}, u32[]{:S(2)}, u32[]{:S(2)}) collective-permute-start(f32[8,192,384]{2,1,0:T(8,128)} %collective-permute-done.2.refs_2_), channel_id=1, source_target_pairs={{0,1},{1,0},{2,3},{3,2},{4,5},{5,4},{6,7},{7,6},{8,9},{9,8},{10,11... | collective-permute-start | bytes 7077896 | tf_op jit(solution)/shard_map/ppermute | solution.py:253
  388.6 15.6 %collective-permute-start.6 = (f32[4,192,384]{2,1,0:T(8,128)S(1)}, f32[4,192,384]{2,1,0:T(8,128)}, u32[]{:S(2)}, u32[]{:S(2)}) collective-permute-start(f32[4,192,384]{2,1,0:T(8,128)S(1)} %collective-permute-done.4.refs_4_), channel_id=1, source_target_pairs={{0,1},{1,0},{2,3},{3,2},{4,5},{5,4},{6,7},{7,6},{8,9},{9,8},{10,11... | collective-permute-start | bytes 3538952 | tf_op jit(solution)/shard_map/ppermute | solution.py:253
  388.7 15.5 %collective-permute-start.9 = (f32[4,192,384]{2,1,0:T(8,128)}, f32[4,192,384]{2,1,0:T(8,128)}, u32[]{:S(2)}, u32[]{:S(2)}) collective-permute-start(f32[4,192,384]{2,1,0:T(8,128)} %copy-done.3), channel_id=1, source_target_pairs={{0,1},{1,0},{2,3},{3,2},{4,5},{5,4},{6,7},{7,6},{8,9},{9,8},{10,11... | collective-permute-start | bytes 3538952 | tf_op jit(solution)/shard_map/ppermute | solution.py:253
  389.1 15.1 %collective-permute-start.11 = (f32[4,192,384]{2,1,0:T(8,128)}, f32[4,192,384]{2,1,0:T(8,128)}, u32[]{:S(2)}, u32[]{:S(2)}) collective-permute-start(f32[4,192,384]{2,1,0:T(8,128)} %copy-done.4), channel_id=1, source_target_pairs={{0,1},{1,0},{2,3},{3,2},{4,5},{5,4},{6,7},{7,6},{8,9},{9,8},{10,11... | collective-permute-start | bytes 3538952 | tf_op jit(solution)/shard_map/ppermute | solution.py:253
  398.1 1.4 copy-start.1
  399.5 4.8 collective-permute-start.8
  404.3 1.0 copy-start.5
  493.1 109.9 %all-to-all-start.5 = ((f32[8,2,192,384]{3,2,1,0:T(8,128)}), f32[8,2,192,384]{3,2,1,0:T(8,128)}, u32[]{:S(2)}, u32[]{:S(2)}) async-start(f32[8,2,192,384]{3,2,1,0:T(8,128)} %block_density.5), calls=%async_computation.5 | async-start | bytes 9437184 | tf_op jit(solution)/shard_map/all_to_all | solution.py:343
  602.9 211.4 %all-to-all-start.4 = ((f32[8,4,192,384]{3,2,1,0:T(8,128)}), f32[8,4,192,384]{3,2,1,0:T(8,128)}, u32[]{:S(2)}, u32[]{:S(2)}) async-start(f32[8,4,192,384]{3,2,1,0:T(8,128)} %block_density.4), calls=%async_computation.4 | async-start | bytes 18874368 | tf_op jit(solution)/shard_map/all_to_all | solution.py:343
  814.4 109.8 %all-to-all-start.3 = ((f32[8,2,192,384]{3,2,1,0:T(8,128)}), f32[8,2,192,384]{3,2,1,0:T(8,128)}, u32[]{:S(2)}, u32[]{:S(2)}) async-start(f32[8,2,192,384]{3,2,1,0:T(8,128)} %block_density.3), calls=%async_computation.3 | async-start | bytes 9437184 | tf_op jit(solution)/shard_map/all_to_all | solution.py:343
